TPU v7x, 128 devices: a whole 4x4x4 slice. The times are simulated.
128 devices in a mesh: seq: 8 (over z, core), grp: 16 (over x, y).
Axes of the slice: x: 4, y: 4, z: 4, core: 2. Of those that a mesh axis runs over, the one named last changes fastest.
Arguments:
- mamba_input: bfloat16 [16, 1024, 8192], P('grp', 'seq'), may hold values from -6 to 6
- gate_input: bfloat16 [16, 1024, 8192], P('grp', 'seq'), may hold values from -6 to 6
- step_raw: bfloat16 [16, 1024, 8192], P('grp', 'seq'), may hold values from -12 to 8
- scan_proj: bfloat16 [16, 2, 16, 1024], P('grp', None, None, 'seq'), may hold values from -3 to 3
- decay_log: float32 [16, 8192], replicated, may hold values from -4 to 7
- step_bias: float32 [8192], replicated, may hold values from -0.5 to 0.5
- conv_weight: float32 [4, 8192], replicated, may hold values from -3 to 3
- conv_bias: float32 [8192], replicated, may hold values from -0.5 to 0.5
- skip_gain: float32 [8192], replicated, may hold values from 0.5 to 1.5
- kv_rows: bfloat16 [16, 1024, 2048], P('grp', 'seq'), may hold values from -6 to 6
- decode_device: int32 [16], replicated, may hold values from 0 to 15, as said below
- block_count: int32 [16], replicated, may hold values from 1 to 64, as said below
- block_slot: int32 [16, 64], replicated, may hold values from 0 to 23, as said below
Outputs:
- block_out: bfloat16 [16, 1024, 8192], P('grp', 'seq')
- kv_cache: bfloat16 [16, 8, 24, 16, 2048], P('grp', 'seq')
- ssm_cache: float32 [16, 3, 16, 8192], P('grp', None, None, 'seq')
- conv_cache: bfloat16 [16, 3, 3, 8192], P('grp', None, None, 'seq')
Inputs may be any that keep to these rules, and one draw needn't show every extreme that they name: `decode_device`: no decode device takes more than 3 requests, and some decode device takes exactly 3. `block_count`: some request has all 64 blocks. `block_slot`: blocks b < block_count of requests with the same decode device and the same b // 8 have distinct slots.
All inputs are finite; a program needn't handle non-finite values.
Results may differ from a plain program's by a relative error of at most 0.013.
Values may be sent and summed in bfloat16 or wider, within the bound.
No kernel may reach another device: no remote copies, remote signals or barrier semaphores. Data moves between devices by JAX's collectives and lax.ppermute only.
A program may use at most 192 MiB of HBM per device.

v0:
```python
import functools

import jax
import jax.numpy as jnp
import numpy as np
from jax import lax
from jax.experimental import pallas as pl
from jax.experimental.pallas import tpu as pltpu
from jax.sharding import PartitionSpec as P

NSTATE = 16
KCONV = 4
BLOCK = 16
MOST = 3
LANES = 128
RIM = 8
LOG2E = 1.4426950408889634
MSG = 32
VMEM_BYTES = 48 * 1024 * 1024
F32 = jnp.float32
BF16 = jnp.bfloat16

VM = functools.partial(pl.BlockSpec, memory_space=pltpu.VMEM)
SM = pl.BlockSpec(memory_space=pltpu.SMEM)


def silu_of_half(h):
    return h + h * jnp.tanh(h)


def split(v):
    high = v.astype(BF16)
    return high, (v - high.astype(F32)).astype(BF16)


def segment_end(count_ref, length):
    return count_ref[lax.axis_index("grp")] * BLOCK - lax.axis_index("seq") * length


def prepare_kernel(
    width, count_ref, step_ref, sbias_ref, proj_ref, tri_ref, dt_ref, run_ref, b_ref, c_ref
):
    length, channels = step_ref.shape
    groups = length // NSTATE
    seg_end = segment_end(count_ref, length)

    @pl.when(pl.program_id(0) == 0)
    def _():
        b_rows = proj_ref[0].astype(F32)
        for t in range(length):
            b_ref[t] = jnp.broadcast_to(b_rows[:, t : t + 1], (NSTATE, LANES))
        wide = NSTATE * NSTATE
        spread = lax.broadcasted_iota(jnp.int32, (NSTATE, wide), 1) % NSTATE
        spread = (spread == lax.broadcasted_iota(jnp.int32, (NSTATE, wide), 0)).astype(BF16)
        tiled = lax.dot_general(
            proj_ref[1], spread, (((0,), (0,)), ((), ())), preferred_element_type=F32
        )
        row = lax.broadcasted_iota(jnp.int32, (length, wide), 0) % NSTATE
        col = lax.broadcasted_iota(jnp.int32, (length, wide), 1) // NSTATE
        c_ref[...] = jnp.where(row == col, tiled, 0.0).astype(BF16).reshape(groups, NSTATE, wide)

    live = lax.broadcasted_iota(jnp.int32, (length, width), 0) < seg_end
    for lane in range(0, channels, width):
        cut = pl.ds(lane, width)
        e = jnp.exp2(step_ref[:, cut].astype(F32) * LOG2E + sbias_ref[:, cut] * LOG2E)
        dt = jnp.where(e < 2e-3, e - 0.5 * e * e, jnp.log(1.0 + e))
        dt = jnp.where(live, dt, 0.0)
        dt_ref[:, :, cut] = dt.reshape(groups, NSTATE, width)
        high, low = split(dt)
        run = jnp.dot(
            tri_ref[...], jnp.concatenate([high, low], axis=0), preferred_element_type=F32
        )
        run_ref[:, :, cut] = run.reshape(groups, NSTATE, width)


def prepare(count, step, sbias, proj, pieces, width=512):
    length, channels = step.shape
    groups = length // NSTATE
    piece = channels // pieces
    tri = np.tril(np.ones((length, length), np.float32))
    tri = jnp.asarray(np.concatenate([tri, tri], axis=1), BF16)
    blocks = pl.BlockSpec((groups, NSTATE, piece), lambda j: (0, 0, j))
    whole = lambda shape: pl.BlockSpec(shape, lambda j: (0,) * len(shape))
    b_shape = (length, NSTATE, LANES)
    c_shape = (groups, NSTATE, NSTATE * NSTATE)
    return pl.pallas_call(
        functools.partial(prepare_kernel, width),
        grid=(pieces,),
        in_specs=[
            SM,
            pl.BlockSpec((length, piece), lambda j: (0, j)),
            pl.BlockSpec((1, piece), lambda j: (0, j)),
            whole(proj.shape),
            whole(tri.shape),
        ],
        out_specs=[blocks, blocks, whole(b_shape), whole(c_shape)],
        out_shape=[
            jax.ShapeDtypeStruct((groups, NSTATE, channels), F32),
            jax.ShapeDtypeStruct((groups, NSTATE, channels), F32),
            jax.ShapeDtypeStruct(b_shape, F32),
            jax.ShapeDtypeStruct(c_shape, BF16),
        ],
        compiler_params=pltpu.CompilerParams(vmem_limit_bytes=VMEM_BYTES),
        cost_estimate=pl.CostEstimate(
            flops=20 * length * channels,
            bytes_accessed=10 * length * channels,
            transcendentals=2 * length * channels,
        ),
        name="prepare",
    )(count, step, sbias, proj, tri)


def scan_kernel(
    width,
    count_ref,
    x_ref,
    halo_ref,
    dt_ref,
    run_ref,
    log_ref,
    cw_ref,
    cbias_ref,
    skip_ref,
    b_ref,
    c_ref,
    shift_ref,
    out_ref,
    msg_ref,
    drive_s,
    rate_s,
):
    length, channels = x_ref.shape
    groups = length // NSTATE
    seg_end = segment_end(count_ref, length)
    held = jnp.logical_and(seg_end >= 1, seg_end <= length).astype(F32)
    tail_at = pl.multiple_of(jnp.clip(seg_end - NSTATE, 0, length - NSTATE), NSTATE)

    for lane in range(0, channels, width):
        cut = pl.ds(lane, width)
        x = x_ref[:, cut]
        moved = jnp.dot(
            shift_ref[...],
            jnp.concatenate([x, halo_ref[:, cut]], axis=0),
            preferred_element_type=F32,
        )
        half_w = 0.5 * cw_ref[:, cut]
        half = 0.5 * cbias_ref[:, cut] + half_w[KCONV - 1 :] * x.astype(F32)
        for k in range(KCONV - 1):
            half = half + half_w[k : k + 1] * moved[k * length : (k + 1) * length]
        driven = silu_of_half(half).reshape(groups, NSTATE, width)
        drive_s[...] = dt_ref[:, :, cut] * driven
        out_ref[:, :, cut] = skip_ref[:, cut] * driven
        rate_s[...] = -LOG2E * jnp.exp(log_ref[:, cut])

        def one_group(i, state):
            rates = rate_s[...]
            mixes = []
            for tt in range(NSTATE):
                dt_now = dt_ref[i, pl.ds(tt, 1), cut]
                drive_now = drive_s[i, pl.ds(tt, 1), :]
                b_now = jnp.concatenate([b_ref[i * NSTATE + tt]] * (width // LANES), axis=1)
                state = jnp.exp2(dt_now * rates) * state + drive_now * b_now
                mixes.append(state.astype(BF16))
            out_ref[i, :, cut] += jnp.dot(
                c_ref[i], jnp.concatenate(mixes, axis=0), preferred_element_type=F32
            )
            return state

        state = lax.fori_loop(0, groups, one_group, jnp.zeros((NSTATE, width), F32))
        msg_ref[0, pl.ds(0, NSTATE), cut] = state.astype(BF16)
        s_high, s_low = split(run_ref[0, pl.ds(NSTATE - 1, 1), cut])
        tail = x_ref[pl.ds(tail_at, NSTATE), cut].astype(F32) * held
        extra = jnp.concatenate(
            [
                s_high.astype(F32),
                s_low.astype(F32),
                tail[NSTATE - (KCONV - 1) :],
                jnp.zeros((MSG - NSTATE - 2 - (KCONV - 1), width), F32),
            ],
            axis=0,
        )
        msg_ref[0, pl.ds(NSTATE, MSG - NSTATE), cut] = extra.astype(BF16)


def local_scan(count, x, halo, dt, run, log, cw, cbias, skip, b_wide, c_diag, pieces, width=512):
    length, channels = x.shape
    groups = length // NSTATE
    piece = channels // pieces
    rim = halo.shape[0]
    shift = np.zeros(((KCONV - 1) * length, length + rim), np.float32)
    for k in range(KCONV - 1):
        for t in range(length):
            source = t - (KCONV - 1) + k
            shift[k * length + t, source if source >= 0 else length + rim + source] = 1.0
    shift = jnp.asarray(shift, BF16)
    per = lambda rows: pl.BlockSpec((rows, piece), lambda j: (0, j))
    blocks = pl.BlockSpec((groups, NSTATE, piece), lambda j: (0, 0, j))
    whole = lambda a: pl.BlockSpec(a.shape, lambda j: (0,) * a.ndim)
    return pl.pallas_call(
        functools.partial(scan_kernel, width),
        grid=(pieces,),
        in_specs=[
            SM,
            per(length),
            per(rim),
            blocks,
            pl.BlockSpec((1, NSTATE, piece), lambda j: (groups - 1, 0, j)),
            per(NSTATE),
            per(KCONV),
            per(1),
            per(1),
            whole(b_wide),
            whole(c_diag),
            whole(shift),
        ],
        out_specs=[blocks, pl.BlockSpec((1, MSG, piece), lambda j: (j, 0, 0))],
        out_shape=[
            jax.ShapeDtypeStruct((groups, NSTATE, channels), F32),
            jax.ShapeDtypeStruct((pieces, MSG, piece), BF16),
        ],
        scratch_shapes=[
            pltpu.VMEM((groups, NSTATE, width), F32),
            pltpu.VMEM((NSTATE, width), F32),
        ],
        compiler_params=pltpu.CompilerParams(vmem_limit_bytes=VMEM_BYTES),
        cost_estimate=pl.CostEstimate(
            flops=8 * length * channels * NSTATE,
            bytes_accessed=12 * length * channels,
            transcendentals=length * channels * NSTATE,
        ),
        name="local_scan",
    )(count, x, halo, dt, run, log, cw, cbias, skip, b_wide, c_diag, shift)


def chain_kernel(dest_ref, got_ref, log_ref, start_ref, final_ref):
    pieces, _, piece = got_ref.shape
    own = pl.ds(pl.multiple_of(lax.axis_index("seq") * piece, piece), piece)
    rates = -LOG2E * jnp.exp(log_ref[:, own])
    state = jnp.zeros((NSTATE, piece), F32)
    tails = jnp.zeros((NSTATE, piece), F32)
    for r in range(pieces):
        start_ref[r] = state.astype(BF16)
        extra = got_ref[r, pl.ds(NSTATE, MSG - NSTATE), :].astype(F32)
        total = extra[0:1] + extra[1:2]
        state = jnp.exp2(total * rates) * state + got_ref[r, pl.ds(0, NSTATE), :].astype(F32)
        tails = tails + extra
    final_ref[...] = jnp.zeros_like(final_ref)
    dest = dest_ref[lax.axis_index("grp")]
    final_ref[dest, pl.ds(0, NSTATE), :] = state.astype(BF16)
    final_ref[dest, pl.ds(NSTATE, MSG - NSTATE), :] = tails.astype(BF16)


def chain(decode_device, got, log, groups):
    pieces, _, piece = got.shape
    return pl.pallas_call(
        chain_kernel,
        in_specs=[SM, VM(), VM()],
        out_specs=[VM(), VM()],
        out_shape=[
            jax.ShapeDtypeStruct((pieces, NSTATE, piece), BF16),
            jax.ShapeDtypeStruct((groups, MSG, piece), BF16),
        ],
        compiler_params=pltpu.CompilerParams(vmem_limit_bytes=VMEM_BYTES),
        name="chain",
    )(decode_device, got, log)


def finish_kernel(
    width, count_ref, start_ref, out_ref, run_ref, log_ref, gate_ref, c_ref, mixed_ref, rate_s, start_s
):
    length, channels = gate_ref.shape
    groups = length // NSTATE
    seg_end = segment_end(count_ref, length)
    for lane in range(0, channels, width):
        cut = pl.ds(lane, width)
        rate_s[...] = -LOG2E * jnp.exp(log_ref[:, cut])
        start_s[...] = start_ref[0, :, cut].astype(F32)

        def one_group(i, carry):
            rates, start = rate_s[...], start_s[...]
            mixes = []
            for tt in range(NSTATE):
                power = run_ref[i, pl.ds(tt, 1), cut] * rates
                mixes.append((jnp.exp2(power) * start).astype(BF16))
            carried = jnp.dot(
                c_ref[i], jnp.concatenate(mixes, axis=0), preferred_element_type=F32
            )
            rows = pl.ds(pl.multiple_of(i * NSTATE, NSTATE), NSTATE)
            gate = silu_of_half(0.5 * gate_ref[rows, cut].astype(F32))
            mixed = (out_ref[i, :, cut] + carried) * gate
            at = lax.broadcasted_iota(jnp.int32, (NSTATE, width), 0) + i * NSTATE
            mixed_ref[rows, cut] = jnp.where(at < seg_end, mixed, 0.0).astype(BF16)
            return carry

        lax.fori_loop(0, groups, one_group, 0)


def finish(count, start, out, run, log, gate, c_diag, width=512):
    length, channels = gate.shape
    groups = length // NSTATE
    pieces, _, piece = start.shape
    per = lambda rows: pl.BlockSpec((rows, piece), lambda j: (0, j))
    blocks = pl.BlockSpec((groups, NSTATE, piece), lambda j: (0, 0, j))
    return pl.pallas_call(
        functools.partial(finish_kernel, width),
        grid=(pieces,),
        in_specs=[
            SM,
            pl.BlockSpec((1, NSTATE, piece), lambda j: (j, 0, 0)),
            blocks,
            blocks,
            per(NSTATE),
            per(length),
            pl.BlockSpec(c_diag.shape, lambda j: (0, 0, 0)),
        ],
        out_specs=per(length),
        out_shape=jax.ShapeDtypeStruct((length, channels), BF16),
        scratch_shapes=[pltpu.VMEM((NSTATE, width), F32), pltpu.VMEM((NSTATE, width), F32)],
        compiler_params=pltpu.CompilerParams(vmem_limit_bytes=VMEM_BYTES),
        cost_estimate=pl.CostEstimate(
            flops=4 * length * channels * NSTATE,
            bytes_accessed=12 * length * channels,
            transcendentals=length * channels * NSTATE,
        ),
        name="finish",
    )(count, start, out, run, log, gate, c_diag)


def caches_kernel(dest_ref, got_ref, state_ref, rows_ref):
    groups = got_ref.shape[0]
    grp_pos = lax.axis_index("grp")
    state_ref[...] = jnp.zeros_like(state_ref)
    rows_ref[...] = jnp.zeros_like(rows_ref)

    def one(g, taken):
        mine = dest_ref[g] == grp_pos

        @pl.when(mine)
        def _():
            state_ref[taken] = got_ref[g, pl.ds(0, NSTATE), :].astype(F32)
            extra = got_ref[g, pl.ds(NSTATE, MSG - NSTATE), :]
            rows_ref[taken] = extra[2 : 2 + KCONV - 1]

        return taken + mine.astype(jnp.int32)

    lax.fori_loop(0, groups, one, jnp.int32(0))


def caches(decode_device, got):
    piece = got.shape[2]
    return pl.pallas_call(
        caches_kernel,
        in_specs=[SM, VM()],
        out_specs=[VM(), VM()],
        out_shape=[
            jax.ShapeDtypeStruct((MOST, NSTATE, piece), F32),
            jax.ShapeDtypeStruct((MOST, KCONV - 1, piece), BF16),
        ],
        compiler_params=pltpu.CompilerParams(vmem_limit_bytes=VMEM_BYTES),
        name="caches",
    )(decode_device, got)


def kv_kernel(here, dest_ref, count_ref, slot_ref, rows_ref, cache_ref, sems):
    groups = rows_ref.shape[0]
    grp_pos = lax.axis_index("grp")
    first = lax.axis_index("seq") * here
    cache_ref[...] = jnp.zeros_like(cache_ref)

    def each(act):
        def request(g, carry):
            @pl.when(dest_ref[g] == grp_pos)
            def _():
                def block(j, carry):
                    slot = slot_ref[g, first + j]
                    act(
                        pltpu.make_async_copy(
                            rows_ref.at[g, j], cache_ref.at[slot], sems.at[slot]
                        )
                    )
                    return carry

                lax.fori_loop(0, jnp.clip(count_ref[g] - first, 0, here), block, 0)

            return carry

        lax.fori_loop(0, groups, request, 0)

    each(lambda copy: copy.start())
    each(lambda copy: copy.wait())


def place_kv(decode_device, block_count, block_slot, rows, here, capacity):
    width = rows.shape[-1]
    return pl.pallas_call(
        functools.partial(kv_kernel, here),
        in_specs=[SM, SM, SM, pl.BlockSpec(memory_space=pl.ANY)],
        out_specs=VM(),
        out_shape=jax.ShapeDtypeStruct((capacity, BLOCK, width), BF16),
        scratch_shapes=[pltpu.SemaphoreType.DMA((capacity,))],
        compiler_params=pltpu.CompilerParams(vmem_limit_bytes=VMEM_BYTES),
        name="place_kv",
    )(decode_device, block_count, block_slot, rows)


def per_device(
    mamba_input,
    gate_input,
    step_raw,
    scan_proj,
    decay_log,
    step_bias,
    conv_weight,
    conv_bias,
    skip_gain,
    kv_rows,
    decode_device,
    block_count,
    block_slot,
):
    seg_len, channels = mamba_input.shape[1:]
    groups = lax.axis_size("grp")
    pieces = lax.axis_size("seq")
    here = seg_len // BLOCK
    x = mamba_input[0]

    kv_all = lax.all_gather(kv_rows[0].reshape(here, BLOCK, kv_rows.shape[2]), "grp")
    halo = lax.ppermute(x[seg_len - RIM :], "seq", [(s, s + 1) for s in range(pieces - 1)])
    dt, run, b_wide, c_diag = prepare(
        block_count, step_raw[0], step_bias[None], scan_proj[0], pieces
    )
    out, msg = local_scan(
        block_count,
        x,
        halo,
        dt,
        run,
        decay_log,
        conv_weight,
        conv_bias[None],
        skip_gain[None],
        b_wide,
        c_diag,
        pieces,
    )
    got = lax.all_to_all(msg, "seq", split_axis=0, concat_axis=0, tiled=True)
    starts, final = chain(decode_device, got, decay_log, groups)
    start = lax.all_to_all(starts, "seq", split_axis=0, concat_axis=0, tiled=True)
    final_got = lax.all_to_all(final, "grp", split_axis=0, concat_axis=0, tiled=True)
    block_out = finish(block_count, start, out, run, decay_log, gate_input[0], c_diag)
    ssm_cache, conv_cache = caches(decode_device, final_got)
    kv_cache = place_kv(decode_device, block_count, block_slot, kv_all, here, MOST * here)
    return block_out[None], kv_cache[None, None], ssm_cache[None], conv_cache[None]


def solution(mesh):
    return jax.shard_map(
        per_device,
        mesh=mesh,
        in_specs=(
            P("grp", "seq", None),
            P("grp", "seq", None),
            P("grp", "seq", None),
            P("grp", None, None, "seq"),
            P(),
            P(),
            P(),
            P(),
            P(),
            P("grp", "seq", None),
            P(),
            P(),
            P(),
        ),
        out_specs=(
            P("grp", "seq", None),
            P("grp", "seq", None, None, None),
            P("grp", None, None, "seq"),
            P("grp", None, None, "seq"),
        ),
        check_vma=False,
    )
```

profile of v0, /device:TPU:0, one launch (start us, length us, event | category | flops | bytes accessed | tf_op | source)
XLA Modules:
  0.0 134.0 jit_solution(1028249363145191669)
XLA Ops:
  7.2 0.0 all-gather.2.cloned.1.call-start
  7.2 0.0 copy-start.5
  7.2 0.0 copy-start.8
  7.2 0.0 copy-start.10
  7.2 0.0 copy-start.11
  7.3 0.0 copy-start.13
  7.3 0.6 all-gather.2.cloned.1.call-update
  7.9 0.0 copy-start
  7.9 0.0 copy-start.1
  7.9 1.1 slice_bitcast_fusion
  9.0 1.3 collective-permute-start
  10.3 0.0 copy-start.4
  10.3 0.6 copy-done.4
  11.0 0.0 copy-start.6
  11.0 1.6 %copy-done.6 = bf16[1,128,8192]{2,1,0:T(8,128)(2,1)S(1)} copy-done((bf16[1,128,8192]{2,1,0:T(8,128)(2,1)S(1)}, bf16[1,128,8192]{2,1,0:T(8,128)(2,1)}, u32[]{:S(2)}) %copy-start.6) | copy-done | bytes 2097176
  12.5 0.0 copy-start.9
  12.5 0.8 copy-done.9
  13.3 0.0 copy-start.12
  13.3 0.7 copy-done.12
  14.0 0.0 copy-start.14
  14.0 0.8 copy-done.14
  14.8 6.9 %prepare.1 = (f32[8,16,8192]{2,1,0:T(8,128)}, f32[8,16,8192]{2,1,0:T(8,128)}, f32[128,16,128]{2,1,0:T(8,128)S(1)}, bf16[8,16,256]{2,1,0:T(8,128)(2,1)S(1)}) custom-call(s32[16]{0:T(128)S(1)} %copy-done.4, bf16[128,8192]{1,0:T(8,128)(2,1)S(1)} %bitcast.15, f32[1,8192]{1,0:T(1,128)S(1)} %bitcast.17, bf16[2,16,128]{2,1,0:T(8,128)(2,1)S(1)} %bitcast.20, ...), custom_call_target="tpu_custom_call" | custom-call | flops 20971520 | bytes 10485760 | tf_op jit(solution)/shard_map/prepare/pallas_call | solution.py:86
  21.7 0.0 collective-permute-done.halo_ref
  21.7 0.0 copy-done.5
  21.7 0.0 copy-done.8
  21.8 0.0 copy-done.10
  21.8 0.0 copy-done.11
  21.8 0.0 copy-done.13
  21.8 0.0 copy-done
  21.8 0.0 copy-done.1
  21.8 0.0 copy-start.3
  21.8 35.0 %local_scan.1 = (f32[8,16,8192]{2,1,0:T(8,128)}, bf16[8,32,1024]{2,1,0:T(8,128)(2,1)S(1)}) custom-call(s32[16]{0:T(128)S(1)} %copy-done.5, bf16[128,8192]{1,0:T(8,128)(2,1)S(1)} %bitcast.14, bf16[8,8192]{1,0:T(8,128)(2,1)S(1)} %collective-permute-done.halo_ref, f32[8,16,8192]{2,1,0:T(8,128)} %get-tuple-element.14.dt_ref, ...), custom_call_target="tpu_custom_call" | custom-call | flops 134217728 | bytes 12582912 | tf_op jit(solution)/shard_map/local_scan/pallas_call | solution.py:199
  56.9 17.3 %all_to_all.15.got_ref = bf16[8,32,1024]{2,1,0:T(8,128)(2,1)S(1)} all-to-all(bf16[8,32,1024]{2,1,0:T(8,128)(2,1)S(1)} %get-tuple-element.18), channel_id=1, replica_groups=mesh['seq'=8,'grp'=16] {'seq'}, dimensions={0} | all-to-all | bytes 1048576 | tf_op jit(solution)/shard_map/all_to_all | solution.py:446
  74.2 0.0 copy-done.3
  74.2 1.8 %chain.1 = (bf16[8,16,1024]{2,1,0:T(8,128)(2,1)S(1)}, bf16[16,32,1024]{2,1,0:T(8,128)(2,1)}) custom-call(s32[16]{0:T(128)S(1)} %copy-done.3, bf16[8,32,1024]{2,1,0:T(8,128)(2,1)S(1)} %all_to_all.15.got_ref, f32[16,8192]{1,0:T(8,128)S(1)} %copy-done), custom_call_target="tpu_custom_call" | custom-call | tf_op jit(solution)/shard_map/chain/pallas_call | solution.py:255
  75.9 9.9 %all_to_all.16.start_ref = bf16[8,16,1024]{2,1,0:T(8,128)(2,1)S(1)} all-to-all(bf16[8,16,1024]{2,1,0:T(8,128)(2,1)S(1)} %get-tuple-element.19), channel_id=1, replica_groups=mesh['seq'=8,'grp'=16] {'seq'}, dimensions={0} | all-to-all | bytes 524288 | tf_op jit(solution)/shard_map/all_to_all | solution.py:448
  85.9 7.0 %all-to-all-start.2 = ((bf16[16,32,1024]{2,1,0:T(8,128)(2,1)}), bf16[16,32,1024]{2,1,0:T(8,128)(2,1)S(1)}, u32[]{:S(2)}, u32[]{:S(2)}) async-start(bf16[16,32,1024]{2,1,0:T(8,128)(2,1)} %get-tuple-element.21), calls=%async_computation.2 | async-start | bytes 2097152 | tf_op jit(solution)/shard_map/all_to_all | solution.py:449
  92.9 0.0 copy-start.7
  92.9 1.6 %copy-done.7 = bf16[1,128,8192]{2,1,0:T(8,128)(2,1)S(1)} copy-done((bf16[1,128,8192]{2,1,0:T(8,128)(2,1)S(1)}, bf16[1,128,8192]{2,1,0:T(8,128)(2,1)}, u32[]{:S(2)}) %copy-start.7) | copy-done | bytes 2097176
  94.5 0.0 copy-start.2
  94.5 27.8 %finish.1 = bf16[128,8192]{1,0:T(8,128)(2,1)} custom-call(s32[16]{0:T(128)S(1)} %copy-done.5, bf16[8,16,1024]{2,1,0:T(8,128)(2,1)S(1)} %all_to_all.16.start_ref, f32[8,16,8192]{2,1,0:T(8,128)} %get-tuple-element.20.out_ref, f32[8,16,8192]{2,1,0:T(8,128)} %get-tuple-element.15.run_ref, f32[16,8192]{1,0:T(8,128)S(1)} %copy-done, ...), custom_call_target="tpu_custom_call" | custom-call | flops 67108864 | bytes 12582912 | tf_op jit(solution)/shard_map/finish/pallas_call | solution.py:304
  122.3 0.0 all-to-all-done.2.got_ref
  122.3 1.5 %caches.1 = (f32[3,16,1024]{2,1,0:T(8,128)}, bf16[3,3,1024]{2,1,0:T(4,128)(2,1)}) custom-call(s32[16]{0:T(128)S(1)} %copy-done.3, bf16[16,32,1024]{2,1,0:T(8,128)(2,1)S(1)} %all-to-all-done.2.got_ref), custom_call_target="tpu_custom_call" | custom-call | tf_op jit(solution)/shard_map/caches/pallas_call | solution.py:351
  123.7 0.0 all-gather.2.cloned.1.call-done.rows_ref
  123.7 0.0 copy-done.2
  123.8 3.3 %place_kv.1 = bf16[24,16,2048]{2,1,0:T(8,128)(2,1)} custom-call(s32[16]{0:T(128)S(1)} %copy-done.3, s32[16]{0:T(128)S(1)} %copy-done.5, s32[16,64]{1,0:T(8,128)S(1)} %copy-done.2, bf16[16,8,16,2048]{3,2,1,0:T(8,128)(2,1)} %all-gather.2.cloned.1.call-done.rows_ref), custom_call_target="tpu_custom_call" | custom-call | tf_op jit(solution)/shard_map/place_kv/pallas_call | solution.py:395
Async XLA Ops:
  7.2 116.6 %all-gather.2.cloned.1.call-start = ((), (), s32[]{:S(2)}) async-start(), calls=%async_computation.3 | async-start | bytes 8912896 | tf_op jit(solution)/shard_map/all_gather | solution.py:427
  7.2 14.5 %copy-start.5 = (s32[16]{0:T(128)S(1)}, s32[16]{0:T(128)}, u32[]{:S(2)}) copy-start(s32[16]{0:T(128)} %count_ref.7) | copy-start | bytes 196
  7.2 14.5 %copy-start.8 = (f32[4,8192]{1,0:T(4,128)S(1)}, f32[4,8192]{1,0:T(4,128)}, u32[]{:S(2)}) copy-start(f32[4,8192]{1,0:T(4,128)} %cw_ref.1) | copy-start | bytes 393220
  7.2 14.5 %copy-start.10 = (f32[8192]{0:T(1024)S(1)}, f32[8192]{0:T(1024)}, u32[]{:S(2)}) copy-start(f32[8192]{0:T(1024)} %param.22) | copy-start | bytes 98308
  7.2 14.5 %copy-start.11 = (f32[8192]{0:T(1024)S(1)}, f32[8192]{0:T(1024)}, u32[]{:S(2)}) copy-start(f32[8192]{0:T(1024)} %param.23) | copy-start | bytes 98308
  7.3 14.5 %copy-start.13 = (bf16[384,136]{1,0:T(8,128)(2,1)S(1)}, bf16[384,136]{1,0:T(8,128)(2,1)}, u32[]{:S(2)}) copy-start(bf16[384,136]{1,0:T(8,128)(2,1)} %constant.5.clone.shift_ref) | copy-start | bytes 313348
  7.9 13.9 %copy-start = (f32[16,8192]{1,0:T(8,128)S(1)}, f32[16,8192]{1,0:T(8,128)}, u32[]{:S(2)}) copy-start(f32[16,8192]{1,0:T(8,128)} %log_ref.5) | copy-start | bytes 1572868
  7.9 13.9 %copy-start.1 = (bf16[1,128,8192]{2,1,0:T(8,128)(2,1)S(1)}, bf16[1,128,8192]{2,1,0:T(8,128)(2,1)}, u32[]{:S(2)}) copy-start(bf16[1,128,8192]{2,1,0:T(8,128)(2,1)} %param.15) | copy-start | bytes 6291460
  9.0 12.8 %collective-permute-start = (bf16[8,8192]{1,0:T(8,128)(2,1)S(1)}, bf16[8,8192]{1,0:T(8,128)(2,1)S(1)}, u32[]{:S(2)}, u32[]{:S(2)}) collective-permute-start(bf16[8,8192]{1,0:T(8,128)(2,1)S(1)} %slice_bitcast_fusion), channel_id=1, source_target_pairs={{0,16},{16,32},{32,48},{48,64},{64,80},{80,96},{96,112},{1,17},{17... | collective-permute-start | bytes 393224 | tf_op jit(solution)/shard_map/ppermute | solution.py:428
  10.3 0.7 copy-start.4
  11.0 1.6 %copy-start.6 = (bf16[1,128,8192]{2,1,0:T(8,128)(2,1)S(1)}, bf16[1,128,8192]{2,1,0:T(8,128)(2,1)}, u32[]{:S(2)}) copy-start(bf16[1,128,8192]{2,1,0:T(8,128)(2,1)} %param.17) | copy-start | bytes 6291460
  12.5 0.8 copy-start.9
  13.3 0.7 copy-start.12
  14.0 0.8 copy-start.14
  21.8 52.4 %copy-start.3 = (s32[16]{0:T(128)S(1)}, s32[16]{0:T(128)}, u32[]{:S(2)}) copy-start(s32[16]{0:T(128)} %dest_ref.5) | copy-start | bytes 196
  85.9 36.4 %all-to-all-start.2 = ((bf16[16,32,1024]{2,1,0:T(8,128)(2,1)}), bf16[16,32,1024]{2,1,0:T(8,128)(2,1)S(1)}, u32[]{:S(2)}, u32[]{:S(2)}) async-start(bf16[16,32,1024]{2,1,0:T(8,128)(2,1)} %get-tuple-element.21), calls=%async_computation.2 | async-start | bytes 2097152 | tf_op jit(solution)/shard_map/all_to_all | solution.py:449
  92.9 1.6 %copy-start.7 = (bf16[1,128,8192]{2,1,0:T(8,128)(2,1)S(1)}, bf16[1,128,8192]{2,1,0:T(8,128)(2,1)}, u32[]{:S(2)}) copy-start(bf16[1,128,8192]{2,1,0:T(8,128)(2,1)} %param.16) | copy-start | bytes 6291460
  94.5 29.2 %copy-start.2 = (s32[16,64]{1,0:T(8,128)S(1)}, s32[16,64]{1,0:T(8,128)}, u32[]{:S(2)}) copy-start(s32[16,64]{1,0:T(8,128)} %slot_ref.1) | copy-start | bytes 12292
Sparse Core Ops, SparseCore 0:
  10.1 73.2 all-gather.1
where the time goes:
time: 135 us; the launch traced here: 134 us
  Pallas kernels  76.3 us (57%)
  blocking collectives  27.2 us (20%)
  between operations  14.2 us (11%)
  starting transfers between devices  8.38 us (6%)
  local copies, waits for them, and re-layouts  7.23 us (5%)
    pallas_call x1, Pallas kernels, local_scan(): pl.pallas_call(functools.partial(scan_kernel, width), grid=(pieces,), in_...  35 us
    pallas_call x1, Pallas kernels, finish(): pl.pallas_call(functools.partial(finish_kernel, width), grid=(pieces,), i...  27.8 us
    all_to_all x1, blocking collectives, per_device(): got = lax.all_to_all(msg, 'seq', split_axis=0, concat_axis=0, tiled=True)  17.3 us
    all_to_all x1, blocking collectives, per_device(): lax.all_to_all(starts, 'seq', split_axis=0, concat_axis=0, tiled=True)  9.93 us
    all_to_all x1, starting transfers between devices, per_device(): lax.all_to_all(final, 'grp', split_axis=0, concat_axis=0, tiled=True)  7.05 us
    pallas_call x1, Pallas kernels, prepare(): pl.pallas_call(functools.partial(prepare_kernel, width), grid=(pieces,),...  6.9 us
    unnamed x30, local copies, waits for them, and re-layouts  6.16 us
    pallas_call x1, Pallas kernels, place_kv(): pl.pallas_call(functools.partial(kv_kernel, here), in_specs=[SM, SM, SM,...  3.34 us
  transfers between devices with their start and end apart: 3, of which 0 were waited for; matrix products, arithmetic and copies ran while one was open for 1% of the time, Pallas kernels for 54%

commit v1 on v0

--- a/solution.py
+++ b/solution.py
@@ -15,8 +15,8 @@
 LANES = 128
 RIM = 8
 LOG2E = 1.4426950408889634
-MSG = 32
-VMEM_BYTES = 48 * 1024 * 1024
+MSG = 24
+VMEM_BYTES = 62 * 1024 * 1024
 F32 = jnp.float32
 BF16 = jnp.bfloat16
 
@@ -166,12 +166,12 @@
             )
             return state
 
-        state = lax.fori_loop(0, groups, one_group, jnp.zeros((NSTATE, width), F32))
-        msg_ref[0, pl.ds(0, NSTATE), cut] = state.astype(BF16)
+        state = lax.fori_loop(0, groups, one_group, jnp.zeros((NSTATE, width), F32), unroll=True)
         s_high, s_low = split(run_ref[0, pl.ds(NSTATE - 1, 1), cut])
         tail = x_ref[pl.ds(tail_at, NSTATE), cut].astype(F32) * held
-        extra = jnp.concatenate(
+        message = jnp.concatenate(
             [
+                state,
                 s_high.astype(F32),
                 s_low.astype(F32),
                 tail[NSTATE - (KCONV - 1) :],
@@ -179,7 +179,7 @@
             ],
             axis=0,
         )
-        msg_ref[0, pl.ds(NSTATE, MSG - NSTATE), cut] = extra.astype(BF16)
+        msg_ref[0, :, cut] = message.astype(BF16)
 
 
 def local_scan(count, x, halo, dt, run, log, cw, cbias, skip, b_wide, c_diag, pieces, width=512):
@@ -237,17 +237,16 @@
     own = pl.ds(pl.multiple_of(lax.axis_index("seq") * piece, piece), piece)
     rates = -LOG2E * jnp.exp(log_ref[:, own])
     state = jnp.zeros((NSTATE, piece), F32)
-    tails = jnp.zeros((NSTATE, piece), F32)
+    tails = jnp.zeros((MSG - NSTATE, piece), F32)
     for r in range(pieces):
         start_ref[r] = state.astype(BF16)
-        extra = got_ref[r, pl.ds(NSTATE, MSG - NSTATE), :].astype(F32)
-        total = extra[0:1] + extra[1:2]
-        state = jnp.exp2(total * rates) * state + got_ref[r, pl.ds(0, NSTATE), :].astype(F32)
-        tails = tails + extra
+        got = got_ref[r].astype(F32)
+        total = got[NSTATE : NSTATE + 1] + got[NSTATE + 1 : NSTATE + 2]
+        state = jnp.exp2(total * rates) * state + got[:NSTATE]
+        tails = tails + got[NSTATE:]
     final_ref[...] = jnp.zeros_like(final_ref)
     dest = dest_ref[lax.axis_index("grp")]
-    final_ref[dest, pl.ds(0, NSTATE), :] = state.astype(BF16)
-    final_ref[dest, pl.ds(NSTATE, MSG - NSTATE), :] = tails.astype(BF16)
+    final_ref[dest] = jnp.concatenate([state, tails], axis=0).astype(BF16)
 
 
 def chain(decode_device, got, log, groups):
@@ -274,14 +273,14 @@
     for lane in range(0, channels, width):
         cut = pl.ds(lane, width)
         rate_s[...] = -LOG2E * jnp.exp(log_ref[:, cut])
-        start_s[...] = start_ref[0, :, cut].astype(F32)
+        start_s[...] = start_ref[0, :, cut]
 
         def one_group(i, carry):
             rates, start = rate_s[...], start_s[...]
             mixes = []
             for tt in range(NSTATE):
-                power = run_ref[i, pl.ds(tt, 1), cut] * rates
-                mixes.append((jnp.exp2(power) * start).astype(BF16))
+                power = (run_ref[i, pl.ds(tt, 1), cut] * rates).astype(BF16)
+                mixes.append(jnp.exp2(power) * start)
             carried = jnp.dot(
                 c_ref[i], jnp.concatenate(mixes, axis=0), preferred_element_type=F32
             )
@@ -292,7 +291,7 @@
             mixed_ref[rows, cut] = jnp.where(at < seg_end, mixed, 0.0).astype(BF16)
             return carry
 
-        lax.fori_loop(0, groups, one_group, 0)
+        lax.fori_loop(0, groups, one_group, 0, unroll=True)
 
 
 def finish(count, start, out, run, log, gate, c_diag, width=512):
@@ -315,7 +314,7 @@
         ],
         out_specs=per(length),
         out_shape=jax.ShapeDtypeStruct((length, channels), BF16),
-        scratch_shapes=[pltpu.VMEM((NSTATE, width), F32), pltpu.VMEM((NSTATE, width), F32)],
+        scratch_shapes=[pltpu.VMEM((NSTATE, width), F32), pltpu.VMEM((NSTATE, width), BF16)],
         compiler_params=pltpu.CompilerParams(vmem_limit_bytes=VMEM_BYTES),
         cost_estimate=pl.CostEstimate(
             flops=4 * length * channels * NSTATE,
@@ -337,9 +336,9 @@
 
         @pl.when(mine)
         def _():
-            state_ref[taken] = got_ref[g, pl.ds(0, NSTATE), :].astype(F32)
-            extra = got_ref[g, pl.ds(NSTATE, MSG - NSTATE), :]
-            rows_ref[taken] = extra[2 : 2 + KCONV - 1]
+            got = got_ref[g].astype(F32)
+            state_ref[taken] = got[:NSTATE]
+            rows_ref[taken] = got[NSTATE + 2 : NSTATE + 1 + KCONV].astype(BF16)
 
         return taken + mine.astype(jnp.int32)
 

time: 135 us -> 108 us (0.80)
  Pallas kernels: 76.3 us -> 50.7 us
  local copies, waits for them, and re-layouts: 7.23 us -> 2.45 us
  waiting for transfers between devices: 0.63 us -> 2.9 us
    pallas_call x1, Pallas kernels: 27.8 us -> 13.1 us  [finish(): pl.pallas_call(functools.partial(finish_kernel, width), grid=(pieces,), i...]
    pallas_call x1, Pallas kernels: 35 us -> 22.2 us  [local_scan(): pl.pallas_call(functools.partial(scan_kernel, width), grid=(pieces,), in_...]
    unnamed x30 -> x4, local copies, waits for them, and re-layouts: 6.16 us -> 1.53 us
    all_to_all x1, waiting for transfers between devices: 0.01 us -> 2.22 us  [per_device(): lax.all_to_all(final, 'grp', split_axis=0, concat_axis=0, tiled=True)]
    all_to_all x1, blocking collectives: 9.93 us -> 11.6 us  [per_device(): lax.all_to_all(starts, 'seq', split_axis=0, concat_axis=0, tiled=True)]
    pallas_call x1, Pallas kernels: 6.9 us -> 8.31 us  [prepare(): pl.pallas_call(functools.partial(prepare_kernel, width), grid=(pieces,),...]
  transfers between devices with their start and end apart: 3 -> 3, of which waited for: 0 -> 1; matrix products, arithmetic and copies ran while one was open for 1% -> 1% of each run, Pallas kernels for 54% -> 45%
where the time goes in v1:
time: 108 us; the launch traced here: 106 us
  Pallas kernels  50.7 us (47%)
  blocking collectives  28 us (26%)
  between operations  14.1 us (13%)
  starting transfers between devices  8.33 us (8%)
  waiting for transfers between devices  2.9 us (3%)
  local copies, waits for them, and re-layouts  2.45 us (2%)
    pallas_call x1, Pallas kernels, local_scan(): pl.pallas_call(functools.partial(scan_kernel, width), grid=(pieces,), in_...  22.2 us
    all_to_all x1, blocking collectives, per_device(): got = lax.all_to_all(msg, 'seq', split_axis=0, concat_axis=0, tiled=True)  16.4 us
    pallas_call x1, Pallas kernels, finish(): pl.pallas_call(functools.partial(finish_kernel, width), grid=(pieces,), i...  13.1 us
    all_to_all x1, blocking collectives, per_device(): lax.all_to_all(starts, 'seq', split_axis=0, concat_axis=0, tiled=True)  11.6 us
    pallas_call x1, Pallas kernels, prepare(): pl.pallas_call(functools.partial(prepare_kernel, width), grid=(pieces,),...  8.31 us
    all_to_all x1, starting transfers between devices, per_device(): lax.all_to_all(final, 'grp', split_axis=0, concat_axis=0, tiled=True)  6.99 us
    pallas_call x1, Pallas kernels, place_kv(): pl.pallas_call(functools.partial(kv_kernel, here), in_specs=[SM, SM, SM,...  2.71 us
    pallas_call x1, Pallas kernels, chain(): pl.pallas_call(chain_kernel, in_specs=[SM, VM(), VM()], out_specs=[VM(),...  2.35 us
  transfers between devices with their start and end apart: 3, of which 1 were waited for; matrix products, arithmetic and copies ran while one was open for 1% of the time, Pallas kernels for 45%

profile of v1, /device:TPU:0, one launch (start us, length us, event | category | flops | bytes accessed | tf_op | source)
XLA Modules:
  0.0 106.4 jit_solution(12972310062097283103)
XLA Ops:
  7.2 0.0 all-gather.2.cloned.1.call-start
  7.2 0.7 all-gather.2.cloned.1.call-update
  7.9 0.9 slice_bitcast_fusion
  8.8 1.3 %collective-permute-start = (bf16[8,8192]{1,0:T(8,128)(2,1)S(1)}, bf16[8,8192]{1,0:T(8,128)(2,1)S(1)}, u32[]{:S(2)}, u32[]{:S(2)}) collective-permute-start(bf16[8,8192]{1,0:T(8,128)(2,1)S(1)} %slice_bitcast_fusion), channel_id=1, source_target_pairs={{0,16},{16,32},{32,48},{48,64},{64,80},{80,96},{96,112},{1,17},{17... | collective-permute-start | bytes 393224 | tf_op jit(solution)/shard_map/ppermute | solution.py:427
  10.1 8.3 %prepare.1 = (f32[8,16,8192]{2,1,0:T(8,128)}, f32[8,16,8192]{2,1,0:T(8,128)}, f32[128,16,128]{2,1,0:T(8,128)}, bf16[8,16,256]{2,1,0:T(8,128)(2,1)}) custom-call(s32[16]{0:T(128)} %count_ref.7, bf16[128,8192]{1,0:T(8,128)(2,1)} %bitcast.17, f32[1,8192]{1,0:T(1,128)} %bitcast.20, bf16[2,16,128]{2,1,0:T(8,128)(2,1)} %bitcast.24, ...), custom_call_target="tpu_custom_call" | custom-call | flops 20971520 | bytes 10485760 | tf_op jit(solution)/shard_map/prepare/pallas_call | solution.py:86
  18.4 0.0 collective-permute-done.halo_ref
  18.4 0.0 copy-start.1
  18.4 0.6 copy-done.1
  19.1 22.2 %local_scan.1 = (f32[8,16,8192]{2,1,0:T(8,128)}, bf16[8,24,1024]{2,1,0:T(8,128)(2,1)}) custom-call(s32[16]{0:T(128)} %count_ref.7, bf16[128,8192]{1,0:T(8,128)(2,1)} %bitcast.16, bf16[8,8192]{1,0:T(8,128)(2,1)} %copy-done.1, f32[8,16,8192]{2,1,0:T(8,128)} %get-tuple-element.14.dt_ref, f32[8,16,8192]{2,1,0:T(8,128)} %get-tuple-element.15.run_ref, ...), custom_call_target="tpu_custom_call" | custom-call | flops 134217728 | bytes 12582912 | tf_op jit(solution)/shard_map/local_scan/pallas_call | solution.py:199
  41.3 16.4 %all_to_all.15.got_ref = bf16[8,24,1024]{2,1,0:T(8,128)(2,1)} all-to-all(bf16[8,24,1024]{2,1,0:T(8,128)(2,1)} %get-tuple-element.18), channel_id=1, replica_groups=mesh['seq'=8,'grp'=16] {'seq'}, dimensions={0} | all-to-all | bytes 786432 | tf_op jit(solution)/shard_map/all_to_all | solution.py:445
  57.7 2.3 %chain.1 = (bf16[8,16,1024]{2,1,0:T(8,128)(2,1)}, bf16[16,24,1024]{2,1,0:T(8,128)(2,1)}) custom-call(s32[16]{0:T(128)} %dest_ref.5, bf16[8,24,1024]{2,1,0:T(8,128)(2,1)} %all_to_all.15.got_ref, f32[16,8192]{1,0:T(8,128)} %log_ref.5), custom_call_target="tpu_custom_call" | custom-call | tf_op jit(solution)/shard_map/chain/pallas_call | solution.py:254
  60.1 11.6 %all_to_all.16.start_ref = bf16[8,16,1024]{2,1,0:T(8,128)(2,1)} all-to-all(bf16[8,16,1024]{2,1,0:T(8,128)(2,1)} %get-tuple-element.19), channel_id=1, replica_groups=mesh['seq'=8,'grp'=16] {'seq'}, dimensions={0} | all-to-all | bytes 524288 | tf_op jit(solution)/shard_map/all_to_all | solution.py:447
  71.6 7.0 %all-to-all-start.2 = ((bf16[16,24,1024]{2,1,0:T(8,128)(2,1)}), bf16[16,24,1024]{2,1,0:T(8,128)(2,1)S(1)}, u32[]{:S(2)}, u32[]{:S(2)}) async-start(bf16[16,24,1024]{2,1,0:T(8,128)(2,1)} %get-tuple-element.21), calls=%async_computation.2 | async-start | bytes 1572864 | tf_op jit(solution)/shard_map/all_to_all | solution.py:448
  78.6 13.1 %finish.1 = bf16[128,8192]{1,0:T(8,128)(2,1)} custom-call(s32[16]{0:T(128)} %count_ref.7, bf16[8,16,1024]{2,1,0:T(8,128)(2,1)} %all_to_all.16.start_ref, f32[8,16,8192]{2,1,0:T(8,128)} %get-tuple-element.20.out_ref, f32[8,16,8192]{2,1,0:T(8,128)} %get-tuple-element.15.run_ref, f32[16,8192]{1,0:T(8,128)} %log_ref.5, bf16[128,8192]{1,0:T(8,128)(2,1)} %bitcast.18, ...), custom_call_target="tpu_custom_call" | custom-call | flops 67108864 | bytes 12582912 | tf_op jit(solution)/shard_map/finish/pallas_call | solution.py:303
  91.7 2.2 %all-to-all-done.2.got_ref = bf16[16,24,1024]{2,1,0:T(8,128)(2,1)S(1)} async-done(((bf16[16,24,1024]{2,1,0:T(8,128)(2,1)}), bf16[16,24,1024]{2,1,0:T(8,128)(2,1)S(1)}, u32[]{:S(2)}, u32[]{:S(2)}) %all-to-all-start.2) | async-done | bytes 786464 | tf_op jit(solution)/shard_map/all_to_all | solution.py:448
  93.9 0.0 copy-start
  93.9 0.9 copy-done
  94.8 2.1 %caches.1 = (f32[3,16,1024]{2,1,0:T(8,128)}, bf16[3,3,1024]{2,1,0:T(4,128)(2,1)}) custom-call(s32[16]{0:T(128)} %dest_ref.5, bf16[16,24,1024]{2,1,0:T(8,128)(2,1)} %copy-done), custom_call_target="tpu_custom_call" | custom-call | tf_op jit(solution)/shard_map/caches/pallas_call | solution.py:350
  96.9 0.0 all-gather.2.cloned.1.call-done.rows_ref
  96.9 2.7 %place_kv.1 = bf16[24,16,2048]{2,1,0:T(8,128)(2,1)} custom-call(s32[16]{0:T(128)} %dest_ref.5, s32[16]{0:T(128)} %count_ref.7, s32[16,64]{1,0:T(8,128)} %slot_ref.1, bf16[16,8,16,2048]{3,2,1,0:T(8,128)(2,1)} %all-gather.2.cloned.1.call-done.rows_ref), custom_call_target="tpu_custom_call" | custom-call | tf_op jit(solution)/shard_map/place_kv/pallas_call | solution.py:394
Async XLA Ops:
  7.2 89.7 %all-gather.2.cloned.1.call-start = ((), (), s32[]{:S(2)}) async-start(), calls=%async_computation.3 | async-start | bytes 8912896 | tf_op jit(solution)/shard_map/all_gather | solution.py:426
  8.8 9.6 %collective-permute-start = (bf16[8,8192]{1,0:T(8,128)(2,1)S(1)}, bf16[8,8192]{1,0:T(8,128)(2,1)S(1)}, u32[]{:S(2)}, u32[]{:S(2)}) collective-permute-start(bf16[8,8192]{1,0:T(8,128)(2,1)S(1)} %slice_bitcast_fusion), channel_id=1, source_target_pairs={{0,16},{16,32},{32,48},{48,64},{64,80},{80,96},{96,112},{1,17},{17... | collective-permute-start | bytes 393224 | tf_op jit(solution)/shard_map/ppermute | solution.py:427
  18.4 0.7 copy-start.1
  71.6 22.3 %all-to-all-start.2 = ((bf16[16,24,1024]{2,1,0:T(8,128)(2,1)}), bf16[16,24,1024]{2,1,0:T(8,128)(2,1)S(1)}, u32[]{:S(2)}, u32[]{:S(2)}) async-start(bf16[16,24,1024]{2,1,0:T(8,128)(2,1)} %get-tuple-element.21), calls=%async_computation.2 | async-start | bytes 1572864 | tf_op jit(solution)/shard_map/all_to_all | solution.py:448
  93.9 0.9 copy-start
Sparse Core Ops, SparseCore 0:
  10.1 74.5 all-gather.1

commit v2 on v1

v2 whole, which is shorter than its diff:
```python
import functools

import jax
import jax.numpy as jnp
import numpy as np
from jax import lax
from jax.experimental import pallas as pl
from jax.experimental.pallas import tpu as pltpu
from jax.sharding import PartitionSpec as P

NSTATE = 16
KCONV = 4
BLOCK = 16
MOST = 3
LANES = 128
RIM = 8
STEPS = 8
LOG2E = 1.4426950408889634
MSG = 24
VMEM_BYTES = 62 * 1024 * 1024
F32 = jnp.float32
BF16 = jnp.bfloat16

VM = functools.partial(pl.BlockSpec, memory_space=pltpu.VMEM)
SM = pl.BlockSpec(memory_space=pltpu.SMEM)


def silu_of_half(h):
    return h + h * jnp.tanh(h)


def split(v):
    high = v.astype(BF16)
    return high, (v - high.astype(F32)).astype(BF16)


def segment_end(count_ref, length):
    return count_ref[lax.axis_index("grp")] * BLOCK - lax.axis_index("seq") * length


def prepare_kernel(
    width, count_ref, step_ref, sbias_ref, proj_ref, dt_ref, b_ref, c_ref
):
    length, channels = step_ref.shape
    groups = length // NSTATE
    seg_end = segment_end(count_ref, length)

    @pl.when(pl.program_id(0) == 0)
    def _():
        b_rows = proj_ref[0].astype(F32)
        for t in range(length):
            b_ref[t] = jnp.broadcast_to(b_rows[:, t : t + 1], (NSTATE, LANES))
        wide = NSTATE * NSTATE
        spread = lax.broadcasted_iota(jnp.int32, (NSTATE, wide), 1) % NSTATE
        spread = (spread == lax.broadcasted_iota(jnp.int32, (NSTATE, wide), 0)).astype(BF16)
        tiled = lax.dot_general(
            proj_ref[1], spread, (((0,), (0,)), ((), ())), preferred_element_type=F32
        )
        row = lax.broadcasted_iota(jnp.int32, (length, wide), 0) % NSTATE
        col = lax.broadcasted_iota(jnp.int32, (length, wide), 1) // NSTATE
        c_ref[...] = jnp.where(row == col, tiled, 0.0).astype(BF16).reshape(groups, NSTATE, wide)

    live = lax.broadcasted_iota(jnp.int32, (length, width), 0) < seg_end
    for lane in range(0, channels, width):
        cut = pl.ds(lane, width)
        e = jnp.exp2(step_ref[:, cut].astype(F32) * LOG2E + sbias_ref[:, cut] * LOG2E)
        dt = jnp.where(e < 2e-3, e - 0.5 * e * e, jnp.log(1.0 + e))
        dt = jnp.where(live, dt, 0.0)
        dt_ref[:, :, cut] = dt.reshape(groups, NSTATE, width)


def prepare(count, step, sbias, proj, steps, width=512):
    length, channels = step.shape
    groups = length // NSTATE
    piece = channels // steps
    blocks = pl.BlockSpec((groups, NSTATE, piece), lambda j: (0, 0, j))
    whole = lambda shape: pl.BlockSpec(shape, lambda j: (0,) * len(shape))
    b_shape = (length, NSTATE, LANES)
    c_shape = (groups, NSTATE, NSTATE * NSTATE)
    return pl.pallas_call(
        functools.partial(prepare_kernel, width),
        grid=(steps,),
        in_specs=[
            SM,
            pl.BlockSpec((length, piece), lambda j: (0, j)),
            pl.BlockSpec((1, piece), lambda j: (0, j)),
            whole(proj.shape),
        ],
        out_specs=[blocks, whole(b_shape), whole(c_shape)],
        out_shape=[
            jax.ShapeDtypeStruct((groups, NSTATE, channels), F32),
            jax.ShapeDtypeStruct(b_shape, F32),
            jax.ShapeDtypeStruct(c_shape, BF16),
        ],
        compiler_params=pltpu.CompilerParams(vmem_limit_bytes=VMEM_BYTES),
        cost_estimate=pl.CostEstimate(
            flops=20 * length * channels,
            bytes_accessed=10 * length * channels,
            transcendentals=2 * length * channels,
        ),
        name="prepare",
    )(count, step, sbias, proj)


def scan_kernel(
    width,
    count_ref,
    x_ref,
    halo_ref,
    dt_ref,
    log_ref,
    cw_ref,
    cbias_ref,
    skip_ref,
    b_ref,
    c_ref,
    shift_ref,
    tri_ref,
    out_ref,
    run_ref,
    msg_ref,
    drive_s,
    rate_s,
):
    length, channels = x_ref.shape
    groups = length // NSTATE
    seg_end = segment_end(count_ref, length)
    held = jnp.logical_and(seg_end >= 1, seg_end <= length).astype(F32)
    tail_at = pl.multiple_of(jnp.clip(seg_end - NSTATE, 0, length - NSTATE), NSTATE)

    base = pl.program_id(0) * channels
    piece = msg_ref.shape[2]

    def tile(l, carry):
        cut = pl.ds(pl.multiple_of(l * width, width), width)
        at = pl.ds(pl.multiple_of(base + l * width, width), width)
        x = x_ref[:, cut]
        moved = jnp.dot(
            shift_ref[...],
            jnp.concatenate([x, halo_ref[:, at]], axis=0),
            preferred_element_type=F32,
        )
        half_w = 0.5 * cw_ref[:, at]
        half = 0.5 * cbias_ref[:, at] + half_w[KCONV - 1 :] * x.astype(F32)
        for k in range(KCONV - 1):
            half = half + half_w[k : k + 1] * moved[k * length : (k + 1) * length]
        driven = silu_of_half(half).reshape(groups, NSTATE, width)
        dt = dt_ref[:, :, cut]
        drive_s[...] = dt * driven
        high, low = split(dt.reshape(length, width))
        run = jnp.dot(
            tri_ref[...], jnp.concatenate([high, low], axis=0), preferred_element_type=F32
        )
        run_ref[:, :, cut] = run.reshape(groups, NSTATE, width)
        out_ref[:, :, cut] = skip_ref[:, at] * driven
        rate_s[...] = -LOG2E * jnp.exp(log_ref[:, at])

        def one_group(i, state):
            rates = rate_s[...]
            mixes = []
            for tt in range(NSTATE):
                dt_now = dt_ref[i, pl.ds(tt, 1), cut]
                drive_now = drive_s[i, pl.ds(tt, 1), :]
                b_now = jnp.concatenate([b_ref[i * NSTATE + tt]] * (width // LANES), axis=1)
                state = jnp.exp2(dt_now * rates) * state + drive_now * b_now
                mixes.append(state.astype(BF16))
            out_ref[i, :, cut] += jnp.dot(
                c_ref[i], jnp.concatenate(mixes, axis=0), preferred_element_type=F32
            )
            return state

        state = lax.fori_loop(0, groups, one_group, jnp.zeros((NSTATE, width), F32), unroll=True)
        s_high, s_low = split(run[length - 1 :])
        tail = x_ref[pl.ds(tail_at, NSTATE), cut].astype(F32) * held
        message = jnp.concatenate(
            [
                state,
                s_high.astype(F32),
                s_low.astype(F32),
                tail[NSTATE - (KCONV - 1) :],
                jnp.zeros((MSG - NSTATE - 2 - (KCONV - 1), width), F32),
            ],
            axis=0,
        )
        inside = pl.ds(pl.multiple_of((l * width) % piece, width), width)
        msg_ref[(l * width) // piece, :, inside] = message.astype(BF16)
        return carry

    lax.fori_loop(0, channels // width, tile, 0)


def local_scan(
    count, x, halo, dt, log, cw, cbias, skip, b_wide, c_diag, pieces, steps, width=512
):
    length, channels = x.shape
    groups = length // NSTATE
    piece = channels // pieces
    block = channels // steps
    rim = halo.shape[0]
    shift = np.zeros(((KCONV - 1) * length, length + rim), np.float32)
    for k in range(KCONV - 1):
        for t in range(length):
            source = t - (KCONV - 1) + k
            shift[k * length + t, source if source >= 0 else length + rim + source] = 1.0
    shift = jnp.asarray(shift, BF16)
    tri = np.tril(np.ones((length, length), np.float32))
    tri = jnp.asarray(np.concatenate([tri, tri], axis=1), BF16)
    per = lambda rows: pl.BlockSpec((rows, block), lambda j: (0, j))
    blocks = pl.BlockSpec((groups, NSTATE, block), lambda j: (0, 0, j))
    whole = lambda a: pl.BlockSpec(a.shape, lambda j: (0,) * a.ndim)
    return pl.pallas_call(
        functools.partial(scan_kernel, width),
        grid=(steps,),
        in_specs=[
            SM,
            per(length),
            whole(halo),
            blocks,
            whole(log),
            whole(cw),
            whole(cbias),
            whole(skip),
            whole(b_wide),
            whole(c_diag),
            whole(shift),
            whole(tri),
        ],
        out_specs=[blocks, blocks, pl.BlockSpec((block // piece, MSG, piece), lambda j: (j, 0, 0))],
        out_shape=[
            jax.ShapeDtypeStruct((groups, NSTATE, channels), F32),
            jax.ShapeDtypeStruct((groups, NSTATE, channels), F32),
            jax.ShapeDtypeStruct((pieces, MSG, piece), BF16),
        ],
        scratch_shapes=[
            pltpu.VMEM((groups, NSTATE, width), F32),
            pltpu.VMEM((NSTATE, width), F32),
        ],
        compiler_params=pltpu.CompilerParams(vmem_limit_bytes=VMEM_BYTES),
        cost_estimate=pl.CostEstimate(
            flops=8 * length * channels * NSTATE,
            bytes_accessed=12 * length * channels,
            transcendentals=length * channels * NSTATE,
        ),
        name="local_scan",
    )(count, x, halo, dt, log, cw, cbias, skip, b_wide, c_diag, shift, tri)


def chain_kernel(dest_ref, got_ref, log_ref, start_ref, final_ref, log_s, sem):
    pieces, _, piece = got_ref.shape
    own = pl.ds(pl.multiple_of(lax.axis_index("seq") * piece, piece), piece)
    copy = pltpu.make_async_copy(log_ref.at[:, own], log_s, sem)
    copy.start()
    copy.wait()
    rates = -LOG2E * jnp.exp(log_s[...])
    state = jnp.zeros((NSTATE, piece), F32)
    tails = jnp.zeros((MSG - NSTATE, piece), F32)
    for r in range(pieces):
        start_ref[r] = state.astype(BF16)
        got = got_ref[r].astype(F32)
        total = got[NSTATE : NSTATE + 1] + got[NSTATE + 1 : NSTATE + 2]
        state = jnp.exp2(total * rates) * state + got[:NSTATE]
        tails = tails + got[NSTATE:]
    final_ref[...] = jnp.zeros_like(final_ref)
    dest = dest_ref[lax.axis_index("grp")]
    final_ref[dest] = jnp.concatenate([state, tails], axis=0).astype(BF16)


def chain(decode_device, got, log, groups):
    pieces, _, piece = got.shape
    return pl.pallas_call(
        chain_kernel,
        in_specs=[SM, VM(), pl.BlockSpec(memory_space=pl.ANY)],
        out_specs=[VM(), VM()],
        out_shape=[
            jax.ShapeDtypeStruct((pieces, NSTATE, piece), BF16),
            jax.ShapeDtypeStruct((groups, MSG, piece), BF16),
        ],
        scratch_shapes=[pltpu.VMEM((NSTATE, piece), F32), pltpu.SemaphoreType.DMA],
        compiler_params=pltpu.CompilerParams(vmem_limit_bytes=VMEM_BYTES),
        name="chain",
    )(decode_device, got, log)


def finish_kernel(
    width, count_ref, start_ref, out_ref, run_ref, log_ref, gate_ref, c_ref, mixed_ref, rate_s, start_s
):
    length, channels = gate_ref.shape
    groups = length // NSTATE
    seg_end = segment_end(count_ref, length)
    base = pl.program_id(0) * channels
    piece = start_ref.shape[2]

    def tile(l, carry):
        cut = pl.ds(pl.multiple_of(l * width, width), width)
        at = pl.ds(pl.multiple_of(base + l * width, width), width)
        inside = pl.ds(pl.multiple_of((l * width) % piece, width), width)
        rate_s[...] = (-LOG2E * jnp.exp(log_ref[:, at])).astype(BF16)
        start_s[...] = start_ref[(l * width) // piece, :, inside]

        def one_group(i, carry):
            rates, start = rate_s[...], start_s[...]
            mixes = []
            for tt in range(NSTATE):
                run_now = jnp.broadcast_to(run_ref[i, pl.ds(tt, 1), cut], (NSTATE, width))
                mixes.append(jnp.exp2(run_now.astype(BF16) * rates) * start)
            carried = jnp.dot(
                c_ref[i], jnp.concatenate(mixes, axis=0), preferred_element_type=F32
            )
            rows = pl.ds(pl.multiple_of(i * NSTATE, NSTATE), NSTATE)
            gate = silu_of_half(0.5 * gate_ref[rows, cut].astype(F32))
            mixed = (out_ref[i, :, cut] + carried) * gate
            row = lax.broadcasted_iota(jnp.int32, (NSTATE, width), 0) + i * NSTATE
            mixed_ref[rows, cut] = jnp.where(row < seg_end, mixed, 0.0).astype(BF16)
            return carry

        lax.fori_loop(0, groups, one_group, 0, unroll=True)
        return carry

    lax.fori_loop(0, channels // width, tile, 0)


def finish(count, start, out, run, log, gate, c_diag, steps, width=1024):
    length, channels = gate.shape
    groups = length // NSTATE
    pieces, _, piece = start.shape
    block = channels // steps
    per = lambda rows: pl.BlockSpec((rows, block), lambda j: (0, j))
    blocks = pl.BlockSpec((groups, NSTATE, block), lambda j: (0, 0, j))
    return pl.pallas_call(
        functools.partial(finish_kernel, width),
        grid=(steps,),
        in_specs=[
            SM,
            pl.BlockSpec((block // piece, NSTATE, piece), lambda j: (j, 0, 0)),
            blocks,
            blocks,
            pl.BlockSpec(log.shape, lambda j: (0, 0)),
            per(length),
            pl.BlockSpec(c_diag.shape, lambda j: (0, 0, 0)),
        ],
        out_specs=per(length),
        out_shape=jax.ShapeDtypeStruct((length, channels), BF16),
        scratch_shapes=[pltpu.VMEM((NSTATE, width), BF16), pltpu.VMEM((NSTATE, width), BF16)],
        compiler_params=pltpu.CompilerParams(vmem_limit_bytes=VMEM_BYTES),
        cost_estimate=pl.CostEstimate(
            flops=4 * length * channels * NSTATE,
            bytes_accessed=12 * length * channels,
            transcendentals=length * channels * NSTATE,
        ),
        name="finish",
    )(count, start, out, run, log, gate, c_diag)


def caches_kernel(
    here,
    dest_ref,
    count_ref,
    slot_ref,
    kv_ref,
    got_ref,
    cache_ref,
    state_ref,
    rows_ref,
    got_s,
    got_sem,
    kv_sems,
):
    groups = got_ref.shape[0]
    grp_pos = lax.axis_index("grp")
    first = lax.axis_index("seq") * here
    got_copy = pltpu.make_async_copy(got_ref, got_s, got_sem)
    got_copy.start()
    cache_ref[...] = jnp.zeros_like(cache_ref)

    def each_block(act):
        def request(g, carry):
            @pl.when(dest_ref[g] == grp_pos)
            def _():
                def block(j, carry):
                    slot = slot_ref[g, first + j]
                    act(
                        pltpu.make_async_copy(
                            kv_ref.at[g, j], cache_ref.at[slot], kv_sems.at[slot]
                        )
                    )
                    return carry

                lax.fori_loop(0, jnp.clip(count_ref[g] - first, 0, here), block, 0)

            return carry

        lax.fori_loop(0, groups, request, 0)

    each_block(lambda copy: copy.start())
    state_ref[...] = jnp.zeros_like(state_ref)
    rows_ref[...] = jnp.zeros_like(rows_ref)
    got_copy.wait()

    def one(g, taken):
        mine = dest_ref[g] == grp_pos

        @pl.when(mine)
        def _():
            got = got_s[g].astype(F32)
            state_ref[taken] = got[:NSTATE]
            rows_ref[taken] = got[NSTATE + 2 : NSTATE + 1 + KCONV].astype(BF16)

        return taken + mine.astype(jnp.int32)

    lax.fori_loop(0, groups, one, jnp.int32(0))
    each_block(lambda copy: copy.wait())


def caches(decode_device, block_count, block_slot, kv, got, here, capacity):
    piece = got.shape[2]
    width = kv.shape[-1]
    return pl.pallas_call(
        functools.partial(caches_kernel, here),
        in_specs=[
            SM,
            SM,
            SM,
            pl.BlockSpec(memory_space=pl.ANY),
            pl.BlockSpec(memory_space=pl.ANY),
        ],
        out_specs=[VM(), VM(), VM()],
        out_shape=[
            jax.ShapeDtypeStruct((capacity, BLOCK, width), BF16),
            jax.ShapeDtypeStruct((MOST, NSTATE, piece), F32),
            jax.ShapeDtypeStruct((MOST, KCONV - 1, piece), BF16),
        ],
        scratch_shapes=[
            pltpu.VMEM(got.shape, BF16),
            pltpu.SemaphoreType.DMA,
            pltpu.SemaphoreType.DMA((capacity,)),
        ],
        compiler_params=pltpu.CompilerParams(vmem_limit_bytes=VMEM_BYTES),
        name="caches",
    )(decode_device, block_count, block_slot, kv, got)


def per_device(
    mamba_input,
    gate_input,
    step_raw,
    scan_proj,
    decay_log,
    step_bias,
    conv_weight,
    conv_bias,
    skip_gain,
    kv_rows,
    decode_device,
    block_count,
    block_slot,
):
    seg_len, channels = mamba_input.shape[1:]
    groups = lax.axis_size("grp")
    pieces = lax.axis_size("seq")
    here = seg_len // BLOCK
    x = mamba_input[0]

    kv_all = lax.all_gather(kv_rows[0].reshape(here, BLOCK, kv_rows.shape[2]), "grp")
    halo = lax.ppermute(x[seg_len - RIM :], "seq", [(s, s + 1) for s in range(pieces - 1)])
    dt, b_wide, c_diag = prepare(block_count, step_raw[0], step_bias[None], scan_proj[0], 2)
    out, run, msg = local_scan(
        block_count,
        x,
        halo,
        dt,
        decay_log,
        conv_weight,
        conv_bias[None],
        skip_gain[None],
        b_wide,
        c_diag,
        pieces,
        STEPS,
    )
    got = lax.all_to_all(msg, "seq", split_axis=0, concat_axis=0, tiled=True)
    starts, final = chain(decode_device, got, decay_log, groups)
    start = lax.all_to_all(starts, "seq", split_axis=0, concat_axis=0, tiled=True)
    final_got = lax.all_to_all(final, "grp", split_axis=0, concat_axis=0, tiled=True)
    block_out = finish(block_count, start, out, run, decay_log, gate_input[0], c_diag, STEPS)
    kv_cache, ssm_cache, conv_cache = caches(
        decode_device, block_count, block_slot, kv_all, final_got, here, MOST * here
    )
    return block_out[None], kv_cache[None, None], ssm_cache[None], conv_cache[None]


def solution(mesh):
    return jax.shard_map(
        per_device,
        mesh=mesh,
        in_specs=(
            P("grp", "seq", None),
            P("grp", "seq", None),
            P("grp", "seq", None),
            P("grp", None, None, "seq"),
            P(),
            P(),
            P(),
            P(),
            P(),
            P("grp", "seq", None),
            P(),
            P(),
            P(),
        ),
        out_specs=(
            P("grp", "seq", None),
            P("grp", "seq", None, None, None),
            P("grp", None, None, "seq"),
            P("grp", None, None, "seq"),
        ),
        check_vma=False,
    )
```

time: 108 us -> 106 us (0.981)
  Pallas kernels: 50.7 us -> 48.6 us
    pallas_call x6 -> x5, Pallas kernels: 50.7 us -> 48.6 us  [the longest x1 24.1 us: local_scan(): pl.pallas_call(functools.partial(scan_kernel, width), grid=(steps,), in_s...]
  transfers between devices with their start and end apart: 3 -> 3, of which waited for: 1 -> 1; matrix products, arithmetic and copies ran while one was open for 1% -> 1% of each run, Pallas kernels for 45% -> 43%
where the time goes in v2:
time: 106 us; the launch traced here: 105 us
  Pallas kernels  48.6 us (46%)
  blocking collectives  27.8 us (26%)
  between operations  14.1 us (13%)
  starting transfers between devices  8.38 us (8%)
  waiting for transfers between devices  3.82 us (4%)
  local copies, waits for them, and re-layouts  2.52 us (2%)
    pallas_call x1, Pallas kernels, local_scan(): pl.pallas_call(functools.partial(scan_kernel, width), grid=(steps,), in_s...  24.1 us
    all_to_all x1, blocking collectives, per_device(): got = lax.all_to_all(msg, 'seq', split_axis=0, concat_axis=0, tiled=True)  16.2 us
    pallas_call x1, Pallas kernels, finish(): pl.pallas_call(functools.partial(finish_kernel, width), grid=(steps,), in...  13.1 us
    all_to_all x1, blocking collectives, per_device(): lax.all_to_all(starts, 'seq', split_axis=0, concat_axis=0, tiled=True)  11.6 us
    all_to_all x1, starting transfers between devices, per_device(): lax.all_to_all(final, 'grp', split_axis=0, concat_axis=0, tiled=True)  7.05 us
    pallas_call x1, Pallas kernels, prepare(): pl.pallas_call(functools.partial(prepare_kernel, width), grid=(steps,), i...  4.98 us
    pallas_call x1, Pallas kernels, caches(): pl.pallas_call(functools.partial(caches_kernel, here), in_specs=[SM, SM,...  3.37 us
    all_to_all x1, waiting for transfers between devices, per_device(): lax.all_to_all(final, 'grp', split_axis=0, concat_axis=0, tiled=True)  3.13 us
  transfers between devices with their start and end apart: 3, of which 1 were waited for; matrix products, arithmetic and copies ran while one was open for 1% of the time, Pallas kernels for 43%

profile of v2, /device:TPU:0, one launch (start us, length us, event | category | flops | bytes accessed | tf_op | source)
XLA Modules:
  0.0 105.2 jit_solution(13499208895637784302)
XLA Ops:
  7.2 0.0 all-gather.2.cloned.1.call-start
  7.2 0.7 all-gather.2.cloned.1.call-update
  7.9 0.9 slice_bitcast_fusion
  8.8 1.3 %collective-permute-start = (bf16[8,8192]{1,0:T(8,128)(2,1)S(1)}, bf16[8,8192]{1,0:T(8,128)(2,1)S(1)}, u32[]{:S(2)}, u32[]{:S(2)}) collective-permute-start(bf16[8,8192]{1,0:T(8,128)(2,1)S(1)} %slice_bitcast_fusion), channel_id=1, source_target_pairs={{0,16},{16,32},{32,48},{48,64},{64,80},{80,96},{96,112},{1,17},{17... | collective-permute-start | bytes 393224 | tf_op jit(solution)/shard_map/ppermute | solution.py:464
  10.1 5.0 %prepare.1 = (f32[8,16,8192]{2,1,0:T(8,128)}, f32[128,16,128]{2,1,0:T(8,128)}, bf16[8,16,256]{2,1,0:T(8,128)(2,1)}) custom-call(s32[16]{0:T(128)} %count_ref.7, bf16[128,8192]{1,0:T(8,128)(2,1)} %bitcast.16, f32[1,8192]{1,0:T(1,128)} %bitcast.20, bf16[2,16,128]{2,1,0:T(8,128)(2,1)} %bitcast.24), custom_call_target="tpu_custom_call" | custom-call | flops 20971520 | bytes 10485760 | tf_op jit(solution)/shard_map/prepare/pallas_call | solution.py:80
  15.1 0.0 collective-permute-done.halo_ref
  15.1 0.0 copy-start.1
  15.1 0.6 copy-done.1
  15.8 24.1 %local_scan.1 = (f32[8,16,8192]{2,1,0:T(8,128)}, f32[8,16,8192]{2,1,0:T(8,128)}, bf16[8,24,1024]{2,1,0:T(8,128)(2,1)}) custom-call(s32[16]{0:T(128)} %count_ref.7, bf16[128,8192]{1,0:T(8,128)(2,1)} %bitcast.15, bf16[8,8192]{1,0:T(8,128)(2,1)} %copy-done.1, f32[8,16,8192]{2,1,0:T(8,128)} %get-tuple-element.15.dt_ref, f32[16,8192]{1,0:T(8,128)} %log_ref.5, ...), custom_call_target="tpu_custom_call" | custom-call | flops 134217728 | bytes 12582912 | tf_op jit(solution)/shard_map/local_scan/pallas_call | solution.py:211
  39.8 16.2 %all_to_all.15.got_ref = bf16[8,24,1024]{2,1,0:T(8,128)(2,1)} all-to-all(bf16[8,24,1024]{2,1,0:T(8,128)(2,1)} %get-tuple-element.18), channel_id=1, replica_groups=mesh['seq'=8,'grp'=16] {'seq'}, dimensions={0} | all-to-all | bytes 786432 | tf_op jit(solution)/shard_map/all_to_all | solution.py:480
  56.1 3.1 %chain.1 = (bf16[8,16,1024]{2,1,0:T(8,128)(2,1)}, bf16[16,24,1024]{2,1,0:T(8,128)(2,1)}) custom-call(s32[16]{0:T(128)} %dest_ref.3, bf16[8,24,1024]{2,1,0:T(8,128)(2,1)} %all_to_all.15.got_ref, f32[16,8192]{1,0:T(8,128)} %log_ref.5), custom_call_target="tpu_custom_call" | custom-call | tf_op jit(solution)/shard_map/chain/pallas_call | solution.py:270
  59.1 11.6 %all_to_all.16.start_ref = bf16[8,16,1024]{2,1,0:T(8,128)(2,1)} all-to-all(bf16[8,16,1024]{2,1,0:T(8,128)(2,1)} %get-tuple-element.19), channel_id=1, replica_groups=mesh['seq'=8,'grp'=16] {'seq'}, dimensions={0} | all-to-all | bytes 524288 | tf_op jit(solution)/shard_map/all_to_all | solution.py:482
  70.7 7.0 %all-to-all-start.2 = ((bf16[16,24,1024]{2,1,0:T(8,128)(2,1)}), bf16[16,24,1024]{2,1,0:T(8,128)(2,1)S(1)}, u32[]{:S(2)}, u32[]{:S(2)}) async-start(bf16[16,24,1024]{2,1,0:T(8,128)(2,1)} %get-tuple-element.22), calls=%async_computation.2 | async-start | bytes 1572864 | tf_op jit(solution)/shard_map/all_to_all | solution.py:483
  77.7 13.1 %finish.1 = bf16[128,8192]{1,0:T(8,128)(2,1)} custom-call(s32[16]{0:T(128)} %count_ref.7, bf16[8,16,1024]{2,1,0:T(8,128)(2,1)} %all_to_all.16.start_ref, f32[8,16,8192]{2,1,0:T(8,128)} %get-tuple-element.20.out_ref, f32[8,16,8192]{2,1,0:T(8,128)} %get-tuple-element.21.run_ref, f32[16,8192]{1,0:T(8,128)} %log_ref.5, bf16[128,8192]{1,0:T(8,128)(2,1)} %bitcast.17, ...), custom_call_target="tpu_custom_call" | custom-call | flops 67108864 | bytes 12582912 | tf_op jit(solution)/shard_map/finish/pallas_call | solution.py:329
  90.9 3.1 %all-to-all-done.2.got_ref = bf16[16,24,1024]{2,1,0:T(8,128)(2,1)S(1)} async-done(((bf16[16,24,1024]{2,1,0:T(8,128)(2,1)}), bf16[16,24,1024]{2,1,0:T(8,128)(2,1)S(1)}, u32[]{:S(2)}, u32[]{:S(2)}) %all-to-all-start.2) | async-done | bytes 786464 | tf_op jit(solution)/shard_map/all_to_all | solution.py:483
  94.0 0.0 copy-start
  94.0 0.0 all-gather.2.cloned.1.call-done.kv_ref
  94.0 0.9 copy-done
  94.9 3.4 %caches.1 = (bf16[24,16,2048]{2,1,0:T(8,128)(2,1)}, f32[3,16,1024]{2,1,0:T(8,128)}, bf16[3,3,1024]{2,1,0:T(4,128)(2,1)}) custom-call(s32[16]{0:T(128)} %dest_ref.3, s32[16]{0:T(128)} %count_ref.7, s32[16,64]{1,0:T(8,128)} %slot_ref.1, bf16[16,8,16,2048]{3,2,1,0:T(8,128)(2,1)} %all-gather.2.cloned.1.call-done.kv_ref, bf16[16,24,1024]{2,1,0:T(8,128)(2,1)} %copy-done), custom_call_target="tpu_custom_call" | custom-call | tf_op jit(solution)/shard_map/caches/pallas_call | solution.py:417
Async XLA Ops:
  7.2 86.8 %all-gather.2.cloned.1.call-start = ((), (), s32[]{:S(2)}) async-start(), calls=%async_computation.3 | async-start | bytes 8912896 | tf_op jit(solution)/shard_map/all_gather | solution.py:463
  8.8 6.3 %collective-permute-start = (bf16[8,8192]{1,0:T(8,128)(2,1)S(1)}, bf16[8,8192]{1,0:T(8,128)(2,1)S(1)}, u32[]{:S(2)}, u32[]{:S(2)}) collective-permute-start(bf16[8,8192]{1,0:T(8,128)(2,1)S(1)} %slice_bitcast_fusion), channel_id=1, source_target_pairs={{0,16},{16,32},{32,48},{48,64},{64,80},{80,96},{96,112},{1,17},{17... | collective-permute-start | bytes 393224 | tf_op jit(solution)/shard_map/ppermute | solution.py:464
  15.1 0.7 copy-start.1
  70.7 23.3 %all-to-all-start.2 = ((bf16[16,24,1024]{2,1,0:T(8,128)(2,1)}), bf16[16,24,1024]{2,1,0:T(8,128)(2,1)S(1)}, u32[]{:S(2)}, u32[]{:S(2)}) async-start(bf16[16,24,1024]{2,1,0:T(8,128)(2,1)} %get-tuple-element.22), calls=%async_computation.2 | async-start | bytes 1572864 | tf_op jit(solution)/shard_map/all_to_all | solution.py:483
  94.0 1.0 copy-start
Sparse Core Ops, SparseCore 0:
  10.1 75.4 all-gather.1

commit v3 on v2

--- a/solution.py
+++ b/solution.py
@@ -16,8 +16,11 @@
 RIM = 8
 STEPS = 8
 LOG2E = 1.4426950408889634
+LOG2LOG2E = 0.5287663729448977
 MSG = 24
 VMEM_BYTES = 62 * 1024 * 1024
+WIDE_BYTES = 48 * 1024 * 1024
+SMALL_BYTES = 16 * 1024 * 1024
 F32 = jnp.float32
 BF16 = jnp.bfloat16
 
@@ -27,6 +30,10 @@
 
 def silu_of_half(h):
     return h + h * jnp.tanh(h)
+
+
+def rate_of(log):
+    return jnp.exp2(log * LOG2E + LOG2LOG2E)
 
 
 def split(v):
@@ -49,7 +56,7 @@
     def _():
         b_rows = proj_ref[0].astype(F32)
         for t in range(length):
-            b_ref[t] = jnp.broadcast_to(b_rows[:, t : t + 1], (NSTATE, LANES))
+            b_ref[t] = jnp.broadcast_to(-b_rows[:, t : t + 1], (NSTATE, LANES))
         wide = NSTATE * NSTATE
         spread = lax.broadcasted_iota(jnp.int32, (NSTATE, wide), 1) % NSTATE
         spread = (spread == lax.broadcasted_iota(jnp.int32, (NSTATE, wide), 0)).astype(BF16)
@@ -64,9 +71,9 @@
     for lane in range(0, channels, width):
         cut = pl.ds(lane, width)
         e = jnp.exp2(step_ref[:, cut].astype(F32) * LOG2E + sbias_ref[:, cut] * LOG2E)
-        dt = jnp.where(e < 2e-3, e - 0.5 * e * e, jnp.log(1.0 + e))
-        dt = jnp.where(live, dt, 0.0)
-        dt_ref[:, :, cut] = dt.reshape(groups, NSTATE, width)
+        minus_dt = jnp.where(e < 2e-3, e * (0.5 * e - 1.0), -jnp.log(1.0 + e))
+        minus_dt = jnp.where(live, minus_dt, 0.0)
+        dt_ref[:, :, cut] = minus_dt.reshape(groups, NSTATE, width)
 
 
 def prepare(count, step, sbias, proj, steps, width=512):
@@ -153,7 +160,7 @@
         )
         run_ref[:, :, cut] = run.reshape(groups, NSTATE, width)
         out_ref[:, :, cut] = skip_ref[:, at] * driven
-        rate_s[...] = -LOG2E * jnp.exp(log_ref[:, at])
+        rate_s[...] = rate_of(log_ref[:, at])
 
         def one_group(i, state):
             rates = rate_s[...]
@@ -245,13 +252,10 @@
     )(count, x, halo, dt, log, cw, cbias, skip, b_wide, c_diag, shift, tri)
 
 
-def chain_kernel(dest_ref, got_ref, log_ref, start_ref, final_ref, log_s, sem):
+def chain_kernel(dest_ref, got_ref, log_ref, start_ref, final_ref):
     pieces, _, piece = got_ref.shape
     own = pl.ds(pl.multiple_of(lax.axis_index("seq") * piece, piece), piece)
-    copy = pltpu.make_async_copy(log_ref.at[:, own], log_s, sem)
-    copy.start()
-    copy.wait()
-    rates = -LOG2E * jnp.exp(log_s[...])
+    rates = rate_of(log_ref[:, own])
     state = jnp.zeros((NSTATE, piece), F32)
     tails = jnp.zeros((MSG - NSTATE, piece), F32)
     for r in range(pieces):
@@ -269,14 +273,13 @@
     pieces, _, piece = got.shape
     return pl.pallas_call(
         chain_kernel,
-        in_specs=[SM, VM(), pl.BlockSpec(memory_space=pl.ANY)],
+        in_specs=[SM, VM(), VM()],
         out_specs=[VM(), VM()],
         out_shape=[
             jax.ShapeDtypeStruct((pieces, NSTATE, piece), BF16),
             jax.ShapeDtypeStruct((groups, MSG, piece), BF16),
         ],
-        scratch_shapes=[pltpu.VMEM((NSTATE, piece), F32), pltpu.SemaphoreType.DMA],
-        compiler_params=pltpu.CompilerParams(vmem_limit_bytes=VMEM_BYTES),
+        compiler_params=pltpu.CompilerParams(vmem_limit_bytes=SMALL_BYTES),
         name="chain",
     )(decode_device, got, log)
 
@@ -294,7 +297,7 @@
         cut = pl.ds(pl.multiple_of(l * width, width), width)
         at = pl.ds(pl.multiple_of(base + l * width, width), width)
         inside = pl.ds(pl.multiple_of((l * width) % piece, width), width)
-        rate_s[...] = (-LOG2E * jnp.exp(log_ref[:, at])).astype(BF16)
+        rate_s[...] = rate_of(log_ref[:, at]).astype(BF16)
         start_s[...] = start_ref[(l * width) // piece, :, inside]
 
         def one_group(i, carry):
@@ -361,15 +364,11 @@
     cache_ref,
     state_ref,
     rows_ref,
-    got_s,
-    got_sem,
     kv_sems,
 ):
     groups = got_ref.shape[0]
     grp_pos = lax.axis_index("grp")
     first = lax.axis_index("seq") * here
-    got_copy = pltpu.make_async_copy(got_ref, got_s, got_sem)
-    got_copy.start()
     cache_ref[...] = jnp.zeros_like(cache_ref)
 
     def each_block(act):
@@ -394,14 +393,13 @@
     each_block(lambda copy: copy.start())
     state_ref[...] = jnp.zeros_like(state_ref)
     rows_ref[...] = jnp.zeros_like(rows_ref)
-    got_copy.wait()
 
     def one(g, taken):
         mine = dest_ref[g] == grp_pos
 
         @pl.when(mine)
         def _():
-            got = got_s[g].astype(F32)
+            got = got_ref[g].astype(F32)
             state_ref[taken] = got[:NSTATE]
             rows_ref[taken] = got[NSTATE + 2 : NSTATE + 1 + KCONV].astype(BF16)
 
@@ -421,7 +419,7 @@
             SM,
             SM,
             pl.BlockSpec(memory_space=pl.ANY),
-            pl.BlockSpec(memory_space=pl.ANY),
+            VM(),
         ],
         out_specs=[VM(), VM(), VM()],
         out_shape=[
@@ -430,11 +428,9 @@
             jax.ShapeDtypeStruct((MOST, KCONV - 1, piece), BF16),
         ],
         scratch_shapes=[
-            pltpu.VMEM(got.shape, BF16),
-            pltpu.SemaphoreType.DMA,
             pltpu.SemaphoreType.DMA((capacity,)),
         ],
-        compiler_params=pltpu.CompilerParams(vmem_limit_bytes=VMEM_BYTES),
+        compiler_params=pltpu.CompilerParams(vmem_limit_bytes=WIDE_BYTES),
         name="caches",
     )(decode_device, block_count, block_slot, kv, got)
 

time: 106 us -> 103 us (0.972)
  Pallas kernels: 48.6 us -> 45 us
  waiting for transfers between devices: 3.82 us -> 6.16 us
  blocking collectives: 27.8 us -> 26.7 us
    all_to_all x1, waiting for transfers between devices: 3.13 us -> 5.48 us  [per_device(): lax.all_to_all(final, 'grp', split_axis=0, concat_axis=0, tiled=True)]
    pallas_call x1, Pallas kernels: 24.1 us -> 22 us  [local_scan(): pl.pallas_call(functools.partial(scan_kernel, width), grid=(steps,), in_s...]
    pallas_call x1, Pallas kernels: 3.05 us -> 1.63 us  [chain(): pl.pallas_call(chain_kernel, in_specs=[SM, VM(), VM()], out_specs=[VM(),...]
  transfers between devices with their start and end apart: 3 -> 3, of which waited for: 1 -> 1; matrix products, arithmetic and copies ran while one was open for 1% -> 1% of each run, Pallas kernels for 43% -> 41%
where the time goes in v3:
time: 103 us; the launch traced here: 102 us
  Pallas kernels  45 us (44%)
  blocking collectives  26.7 us (26%)
  between operations  14.1 us (14%)
  starting transfers between devices  8.35 us (8%)
  waiting for transfers between devices  6.16 us (6%)
  local copies, waits for them, and re-layouts  1.59 us (2%)
    pallas_call x1, Pallas kernels, local_scan(): pl.pallas_call(functools.partial(scan_kernel, width), grid=(steps,), in_s...  22 us
    all_to_all x1, blocking collectives, per_device(): got = lax.all_to_all(msg, 'seq', split_axis=0, concat_axis=0, tiled=True)  16.1 us
    pallas_call x1, Pallas kernels, finish(): pl.pallas_call(functools.partial(finish_kernel, width), grid=(steps,), in...  13.2 us
    all_to_all x1, blocking collectives, per_device(): lax.all_to_all(starts, 'seq', split_axis=0, concat_axis=0, tiled=True)  10.6 us
    all_to_all x1, starting transfers between devices, per_device(): lax.all_to_all(final, 'grp', split_axis=0, concat_axis=0, tiled=True)  7.01 us
    all_to_all x1, waiting for transfers between devices, per_device(): lax.all_to_all(final, 'grp', split_axis=0, concat_axis=0, tiled=True)  5.48 us
    pallas_call x1, Pallas kernels, prepare(): pl.pallas_call(functools.partial(prepare_kernel, width), grid=(steps,), i...  5.33 us
    pallas_call x1, Pallas kernels, caches(): pl.pallas_call(functools.partial(caches_kernel, here), in_specs=[SM, SM,...  2.9 us
  transfers between devices with their start and end apart: 3, of which 1 were waited for; matrix products, arithmetic and copies ran while one was open for 1% of the time, Pallas kernels for 41%

profile of v3, /device:TPU:0, one launch (start us, length us, event | category | flops | bytes accessed | tf_op | source)
XLA Modules:
  0.0 102.0 jit_solution(15154740174831219370)
XLA Ops:
  7.2 0.0 all-gather.2.cloned.1.call-start
  7.2 0.7 all-gather.2.cloned.1.call-update
  7.9 0.9 slice_bitcast_fusion
  8.8 1.3 %collective-permute-start = (bf16[8,8192]{1,0:T(8,128)(2,1)S(1)}, bf16[8,8192]{1,0:T(8,128)(2,1)S(1)}, u32[]{:S(2)}, u32[]{:S(2)}) collective-permute-start(bf16[8,8192]{1,0:T(8,128)(2,1)S(1)} %slice_bitcast_fusion), channel_id=1, source_target_pairs={{0,16},{16,32},{32,48},{48,64},{64,80},{80,96},{96,112},{1,17},{17... | collective-permute-start | bytes 393224 | tf_op jit(solution)/shard_map/ppermute | solution.py:460
  10.1 5.3 %prepare.1 = (f32[8,16,8192]{2,1,0:T(8,128)}, f32[128,16,128]{2,1,0:T(8,128)}, bf16[8,16,256]{2,1,0:T(8,128)(2,1)}) custom-call(s32[16]{0:T(128)} %count_ref.7, bf16[128,8192]{1,0:T(8,128)(2,1)} %bitcast.16, f32[1,8192]{1,0:T(1,128)} %bitcast.20, bf16[2,16,128]{2,1,0:T(8,128)(2,1)} %bitcast.24), custom_call_target="tpu_custom_call" | custom-call | flops 20971520 | bytes 10485760 | tf_op jit(solution)/shard_map/prepare/pallas_call | solution.py:87
  15.5 0.0 collective-permute-done.halo_ref
  15.5 0.0 copy-start.4
  15.5 0.6 copy-done.4
  16.1 0.0 copy-start
  16.1 0.0 copy-start.2
  16.1 22.0 %local_scan.1 = (f32[8,16,8192]{2,1,0:T(8,128)}, f32[8,16,8192]{2,1,0:T(8,128)}, bf16[8,24,1024]{2,1,0:T(8,128)(2,1)}) custom-call(s32[16]{0:T(128)} %count_ref.7, bf16[128,8192]{1,0:T(8,128)(2,1)} %bitcast.15, bf16[8,8192]{1,0:T(8,128)(2,1)} %copy-done.4, f32[8,16,8192]{2,1,0:T(8,128)} %get-tuple-element.15.dt_ref, f32[16,8192]{1,0:T(8,128)} %log_ref.5, ...), custom_call_target="tpu_custom_call" | custom-call | flops 134217728 | bytes 12582912 | tf_op jit(solution)/shard_map/local_scan/pallas_call | solution.py:218
  38.1 16.1 %all_to_all.15.got_ref = bf16[8,24,1024]{2,1,0:T(8,128)(2,1)S(1)} all-to-all(bf16[8,24,1024]{2,1,0:T(8,128)(2,1)} %get-tuple-element.18), channel_id=1, replica_groups=mesh['seq'=8,'grp'=16] {'seq'}, dimensions={0} | all-to-all | bytes 786432 | tf_op jit(solution)/shard_map/all_to_all | solution.py:476
  54.3 0.0 copy-done
  54.3 0.0 copy-done.2
  54.3 1.6 %chain.1 = (bf16[8,16,1024]{2,1,0:T(8,128)(2,1)S(1)}, bf16[16,24,1024]{2,1,0:T(8,128)(2,1)}) custom-call(s32[16]{0:T(128)S(1)} %copy-done.2, bf16[8,24,1024]{2,1,0:T(8,128)(2,1)S(1)} %all_to_all.15.got_ref, f32[16,8192]{1,0:T(8,128)S(1)} %copy-done), custom_call_target="tpu_custom_call" | custom-call | tf_op jit(solution)/shard_map/chain/pallas_call | solution.py:274
  55.9 10.6 %all_to_all.16.start_ref = bf16[8,16,1024]{2,1,0:T(8,128)(2,1)} all-to-all(bf16[8,16,1024]{2,1,0:T(8,128)(2,1)S(1)} %get-tuple-element.19), channel_id=1, replica_groups=mesh['seq'=8,'grp'=16] {'seq'}, dimensions={0} | all-to-all | bytes 524288 | tf_op jit(solution)/shard_map/all_to_all | solution.py:478
  66.5 7.0 %all-to-all-start.2 = ((bf16[16,24,1024]{2,1,0:T(8,128)(2,1)}), bf16[16,24,1024]{2,1,0:T(8,128)(2,1)S(1)}, u32[]{:S(2)}, u32[]{:S(2)}) async-start(bf16[16,24,1024]{2,1,0:T(8,128)(2,1)} %get-tuple-element.22), calls=%async_computation.2 | async-start | bytes 1572864 | tf_op jit(solution)/shard_map/all_to_all | solution.py:479
  73.5 0.0 copy-start.1
  73.5 0.0 copy-start.3
  73.5 13.2 %finish.1 = bf16[128,8192]{1,0:T(8,128)(2,1)} custom-call(s32[16]{0:T(128)} %count_ref.7, bf16[8,16,1024]{2,1,0:T(8,128)(2,1)} %all_to_all.16.start_ref, f32[8,16,8192]{2,1,0:T(8,128)} %get-tuple-element.20.out_ref, f32[8,16,8192]{2,1,0:T(8,128)} %get-tuple-element.21.run_ref, f32[16,8192]{1,0:T(8,128)} %log_ref.5, bf16[128,8192]{1,0:T(8,128)(2,1)} %bitcast.17, ...), custom_call_target="tpu_custom_call" | custom-call | flops 67108864 | bytes 12582912 | tf_op jit(solution)/shard_map/finish/pallas_call | solution.py:332
  86.7 5.5 %all-to-all-done.2.got_ref = bf16[16,24,1024]{2,1,0:T(8,128)(2,1)S(1)} async-done(((bf16[16,24,1024]{2,1,0:T(8,128)(2,1)}), bf16[16,24,1024]{2,1,0:T(8,128)(2,1)S(1)}, u32[]{:S(2)}, u32[]{:S(2)}) %all-to-all-start.2) | async-done | bytes 786464 | tf_op jit(solution)/shard_map/all_to_all | solution.py:479
  92.2 0.0 all-gather.2.cloned.1.call-done.kv_ref
  92.2 0.0 copy-done.1
  92.2 0.0 copy-done.3
  92.2 2.9 %caches.1 = (bf16[24,16,2048]{2,1,0:T(8,128)(2,1)}, f32[3,16,1024]{2,1,0:T(8,128)}, bf16[3,3,1024]{2,1,0:T(4,128)(2,1)}) custom-call(s32[16]{0:T(128)S(1)} %copy-done.2, s32[16]{0:T(128)S(1)} %copy-done.3, s32[16,64]{1,0:T(8,128)S(1)} %copy-done.1, bf16[16,8,16,2048]{3,2,1,0:T(8,128)(2,1)} %all-gather.2.cloned.1.call-done.kv_ref, ...), custom_call_target="tpu_custom_call" | custom-call | tf_op jit(solution)/shard_map/caches/pallas_call | solution.py:415
Async XLA Ops:
  7.2 85.0 %all-gather.2.cloned.1.call-start = ((), (), s32[]{:S(2)}) async-start(), calls=%async_computation.3 | async-start | bytes 8912896 | tf_op jit(solution)/shard_map/all_gather | solution.py:459
  8.8 6.6 %collective-permute-start = (bf16[8,8192]{1,0:T(8,128)(2,1)S(1)}, bf16[8,8192]{1,0:T(8,128)(2,1)S(1)}, u32[]{:S(2)}, u32[]{:S(2)}) collective-permute-start(bf16[8,8192]{1,0:T(8,128)(2,1)S(1)} %slice_bitcast_fusion), channel_id=1, source_target_pairs={{0,16},{16,32},{32,48},{48,64},{64,80},{80,96},{96,112},{1,17},{17... | collective-permute-start | bytes 393224 | tf_op jit(solution)/shard_map/ppermute | solution.py:460
  15.5 0.7 copy-start.4
  16.1 38.2 %copy-start = (f32[16,8192]{1,0:T(8,128)S(1)}, f32[16,8192]{1,0:T(8,128)}, u32[]{:S(2)}) copy-start(f32[16,8192]{1,0:T(8,128)} %log_ref.5) | copy-start | bytes 1572868
  16.1 38.2 %copy-start.2 = (s32[16]{0:T(128)S(1)}, s32[16]{0:T(128)}, u32[]{:S(2)}) copy-start(s32[16]{0:T(128)} %dest_ref.3) | copy-start | bytes 196
  66.5 25.7 %all-to-all-start.2 = ((bf16[16,24,1024]{2,1,0:T(8,128)(2,1)}), bf16[16,24,1024]{2,1,0:T(8,128)(2,1)S(1)}, u32[]{:S(2)}, u32[]{:S(2)}) async-start(bf16[16,24,1024]{2,1,0:T(8,128)(2,1)} %get-tuple-element.22), calls=%async_computation.2 | async-start | bytes 1572864 | tf_op jit(solution)/shard_map/all_to_all | solution.py:479
  73.5 18.7 %copy-start.1 = (s32[16,64]{1,0:T(8,128)S(1)}, s32[16,64]{1,0:T(8,128)}, u32[]{:S(2)}) copy-start(s32[16,64]{1,0:T(8,128)} %slot_ref.1) | copy-start | bytes 12292
  73.5 18.7 %copy-start.3 = (s32[16]{0:T(128)S(1)}, s32[16]{0:T(128)}, u32[]{:S(2)}) copy-start(s32[16]{0:T(128)} %count_ref.7) | copy-start | bytes 196
Sparse Core Ops, SparseCore 0:
  10.1 79.7 all-gather.1

commit v4 on v3

--- a/solution.py
+++ b/solution.py
@@ -221,7 +221,7 @@
         in_specs=[
             SM,
             per(length),
-            whole(halo),
+            VM(),
             blocks,
             whole(log),
             whole(cw),
@@ -364,24 +364,28 @@
     cache_ref,
     state_ref,
     rows_ref,
-    kv_sems,
+    kv_s,
+    zero_s,
+    used_s,
+    in_sems,
+    out_sems,
 ):
-    groups = got_ref.shape[0]
+    groups, capacity = got_ref.shape[0], cache_ref.shape[0]
     grp_pos = lax.axis_index("grp")
     first = lax.axis_index("seq") * here
-    cache_ref[...] = jnp.zeros_like(cache_ref)
+
+    def clear(c, carry):
+        used_s[c] = 0
+        return carry
+
+    lax.fori_loop(0, capacity, clear, 0)
 
     def each_block(act):
         def request(g, carry):
             @pl.when(dest_ref[g] == grp_pos)
             def _():
                 def block(j, carry):
-                    slot = slot_ref[g, first + j]
-                    act(
-                        pltpu.make_async_copy(
-                            kv_ref.at[g, j], cache_ref.at[slot], kv_sems.at[slot]
-                        )
-                    )
+                    act(g, j, slot_ref[g, first + j])
                     return carry
 
                 lax.fori_loop(0, jnp.clip(count_ref[g] - first, 0, here), block, 0)
@@ -390,7 +394,27 @@
 
         lax.fori_loop(0, groups, request, 0)
 
-    each_block(lambda copy: copy.start())
+    def into(g, j, slot):
+        return pltpu.make_async_copy(kv_ref.at[g, j], kv_s.at[slot], in_sems.at[slot])
+
+    def out_of(source, slot):
+        return pltpu.make_async_copy(source, cache_ref.at[slot], out_sems.at[slot])
+
+    def fetch(g, j, slot):
+        used_s[slot] = 1
+        into(g, j, slot).start()
+
+    each_block(fetch)
+    zero_s[...] = jnp.zeros_like(zero_s)
+
+    def fill(c, carry):
+        @pl.when(used_s[c] == 0)
+        def _():
+            out_of(zero_s, c).start()
+
+        return carry
+
+    lax.fori_loop(0, capacity, fill, 0)
     state_ref[...] = jnp.zeros_like(state_ref)
     rows_ref[...] = jnp.zeros_like(rows_ref)
 
@@ -406,7 +430,18 @@
         return taken + mine.astype(jnp.int32)
 
     lax.fori_loop(0, groups, one, jnp.int32(0))
-    each_block(lambda copy: copy.wait())
+
+    def forward(g, j, slot):
+        into(g, j, slot).wait()
+        out_of(kv_s.at[slot], slot).start()
+
+    each_block(forward)
+
+    def ended(c, carry):
+        out_of(zero_s, c).wait()
+        return carry
+
+    lax.fori_loop(0, capacity, ended, 0)
 
 
 def caches(decode_device, block_count, block_slot, kv, got, here, capacity):
@@ -421,13 +456,17 @@
             pl.BlockSpec(memory_space=pl.ANY),
             VM(),
         ],
-        out_specs=[VM(), VM(), VM()],
+        out_specs=[pl.BlockSpec(memory_space=pl.ANY), VM(), VM()],
         out_shape=[
             jax.ShapeDtypeStruct((capacity, BLOCK, width), BF16),
             jax.ShapeDtypeStruct((MOST, NSTATE, piece), F32),
             jax.ShapeDtypeStruct((MOST, KCONV - 1, piece), BF16),
         ],
         scratch_shapes=[
+            pltpu.VMEM((capacity, BLOCK, width), BF16),
+            pltpu.VMEM((BLOCK, width), BF16),
+            pltpu.SMEM((capacity,), jnp.int32),
+            pltpu.SemaphoreType.DMA((capacity,)),
             pltpu.SemaphoreType.DMA((capacity,)),
         ],
         compiler_params=pltpu.CompilerParams(vmem_limit_bytes=WIDE_BYTES),

time: 103 us -> 104 us (level)
  no operation moved by 1% of the time
where the time goes in v4:
time: 104 us; the launch traced here: 102 us
  Pallas kernels  45.4 us (44%)
  blocking collectives  26.7 us (26%)
  between operations  14.1 us (14%)
  starting transfers between devices  8.35 us (8%)
  waiting for transfers between devices  6.16 us (6%)
  local copies, waits for them, and re-layouts  1.59 us (2%)
    pallas_call x1, Pallas kernels, local_scan(): pl.pallas_call(functools.partial(scan_kernel, width), grid=(steps,), in_s...  22 us
    all_to_all x1, blocking collectives, per_device(): got = lax.all_to_all(msg, 'seq', split_axis=0, concat_axis=0, tiled=True)  16.1 us
    pallas_call x1, Pallas kernels, finish(): pl.pallas_call(functools.partial(finish_kernel, width), grid=(steps,), in...  13.2 us
    all_to_all x1, blocking collectives, per_device(): lax.all_to_all(starts, 'seq', split_axis=0, concat_axis=0, tiled=True)  10.6 us
    all_to_all x1, starting transfers between devices, per_device(): lax.all_to_all(final, 'grp', split_axis=0, concat_axis=0, tiled=True)  7.01 us
    all_to_all x1, waiting for transfers between devices, per_device(): lax.all_to_all(final, 'grp', split_axis=0, concat_axis=0, tiled=True)  5.48 us
    pallas_call x1, Pallas kernels, prepare(): pl.pallas_call(functools.partial(prepare_kernel, width), grid=(steps,), i...  5.33 us
    pallas_call x1, Pallas kernels, caches(): pl.pallas_call(functools.partial(caches_kernel, here), in_specs=[SM, SM,...  3.29 us
  transfers between devices with their start and end apart: 3, of which 1 were waited for; matrix products, arithmetic and copies ran while one was open for 1% of the time, Pallas kernels for 41%

profile of v4, /device:TPU:0, one launch (start us, length us, event | category | flops | bytes accessed | tf_op | source)
XLA Modules:
  0.0 102.4 jit_solution(12501901173203300599)
XLA Ops:
  7.2 0.0 all-gather.2.cloned.1.call-start
  7.2 0.7 all-gather.2.cloned.1.call-update
  7.9 0.9 slice_bitcast_fusion
  8.8 1.3 %collective-permute-start = (bf16[8,8192]{1,0:T(8,128)(2,1)S(1)}, bf16[8,8192]{1,0:T(8,128)(2,1)S(1)}, u32[]{:S(2)}, u32[]{:S(2)}) collective-permute-start(bf16[8,8192]{1,0:T(8,128)(2,1)S(1)} %slice_bitcast_fusion), channel_id=1, source_target_pairs={{0,16},{16,32},{32,48},{48,64},{64,80},{80,96},{96,112},{1,17},{17... | collective-permute-start | bytes 393224 | tf_op jit(solution)/shard_map/ppermute | solution.py:499
  10.1 5.3 %prepare.1 = (f32[8,16,8192]{2,1,0:T(8,128)}, f32[128,16,128]{2,1,0:T(8,128)}, bf16[8,16,256]{2,1,0:T(8,128)(2,1)}) custom-call(s32[16]{0:T(128)} %count_ref.7, bf16[128,8192]{1,0:T(8,128)(2,1)} %bitcast.16, f32[1,8192]{1,0:T(1,128)} %bitcast.20, bf16[2,16,128]{2,1,0:T(8,128)(2,1)} %bitcast.24), custom_call_target="tpu_custom_call" | custom-call | flops 20971520 | bytes 10485760 | tf_op jit(solution)/shard_map/prepare/pallas_call | solution.py:87
  15.5 0.0 collective-permute-done.halo_ref
  15.5 0.0 copy-start.4
  15.5 0.6 copy-done.4
  16.1 0.0 copy-start
  16.1 0.0 copy-start.2
  16.1 22.0 %local_scan.1 = (f32[8,16,8192]{2,1,0:T(8,128)}, f32[8,16,8192]{2,1,0:T(8,128)}, bf16[8,24,1024]{2,1,0:T(8,128)(2,1)}) custom-call(s32[16]{0:T(128)} %count_ref.7, bf16[128,8192]{1,0:T(8,128)(2,1)} %bitcast.15, bf16[8,8192]{1,0:T(8,128)(2,1)} %copy-done.4, f32[8,16,8192]{2,1,0:T(8,128)} %get-tuple-element.15.dt_ref, f32[16,8192]{1,0:T(8,128)} %log_ref.5, ...), custom_call_target="tpu_custom_call" | custom-call | flops 134217728 | bytes 12582912 | tf_op jit(solution)/shard_map/local_scan/pallas_call | solution.py:218
  38.1 16.1 %all_to_all.15.got_ref = bf16[8,24,1024]{2,1,0:T(8,128)(2,1)S(1)} all-to-all(bf16[8,24,1024]{2,1,0:T(8,128)(2,1)} %get-tuple-element.18), channel_id=1, replica_groups=mesh['seq'=8,'grp'=16] {'seq'}, dimensions={0} | all-to-all | bytes 786432 | tf_op jit(solution)/shard_map/all_to_all | solution.py:515
  54.3 0.0 copy-done
  54.3 0.0 copy-done.2
  54.3 1.6 %chain.1 = (bf16[8,16,1024]{2,1,0:T(8,128)(2,1)S(1)}, bf16[16,24,1024]{2,1,0:T(8,128)(2,1)}) custom-call(s32[16]{0:T(128)S(1)} %copy-done.2, bf16[8,24,1024]{2,1,0:T(8,128)(2,1)S(1)} %all_to_all.15.got_ref, f32[16,8192]{1,0:T(8,128)S(1)} %copy-done), custom_call_target="tpu_custom_call" | custom-call | tf_op jit(solution)/shard_map/chain/pallas_call | solution.py:274
  55.9 10.6 %all_to_all.16.start_ref = bf16[8,16,1024]{2,1,0:T(8,128)(2,1)} all-to-all(bf16[8,16,1024]{2,1,0:T(8,128)(2,1)S(1)} %get-tuple-element.19), channel_id=1, replica_groups=mesh['seq'=8,'grp'=16] {'seq'}, dimensions={0} | all-to-all | bytes 524288 | tf_op jit(solution)/shard_map/all_to_all | solution.py:517
  66.5 7.0 %all-to-all-start.2 = ((bf16[16,24,1024]{2,1,0:T(8,128)(2,1)}), bf16[16,24,1024]{2,1,0:T(8,128)(2,1)S(1)}, u32[]{:S(2)}, u32[]{:S(2)}) async-start(bf16[16,24,1024]{2,1,0:T(8,128)(2,1)} %get-tuple-element.22), calls=%async_computation.2 | async-start | bytes 1572864 | tf_op jit(solution)/shard_map/all_to_all | solution.py:518
  73.5 0.0 copy-start.1
  73.5 0.0 copy-start.3
  73.5 13.2 %finish.1 = bf16[128,8192]{1,0:T(8,128)(2,1)} custom-call(s32[16]{0:T(128)} %count_ref.7, bf16[8,16,1024]{2,1,0:T(8,128)(2,1)} %all_to_all.16.start_ref, f32[8,16,8192]{2,1,0:T(8,128)} %get-tuple-element.20.out_ref, f32[8,16,8192]{2,1,0:T(8,128)} %get-tuple-element.21.run_ref, f32[16,8192]{1,0:T(8,128)} %log_ref.5, bf16[128,8192]{1,0:T(8,128)(2,1)} %bitcast.17, ...), custom_call_target="tpu_custom_call" | custom-call | flops 67108864 | bytes 12582912 | tf_op jit(solution)/shard_map/finish/pallas_call | solution.py:332
  86.7 5.5 %all-to-all-done.2.got_ref = bf16[16,24,1024]{2,1,0:T(8,128)(2,1)S(1)} async-done(((bf16[16,24,1024]{2,1,0:T(8,128)(2,1)}), bf16[16,24,1024]{2,1,0:T(8,128)(2,1)S(1)}, u32[]{:S(2)}, u32[]{:S(2)}) %all-to-all-start.2) | async-done | bytes 786464 | tf_op jit(solution)/shard_map/all_to_all | solution.py:518
  92.2 0.0 all-gather.2.cloned.1.call-done.kv_ref
  92.2 0.0 copy-done.1
  92.2 0.0 copy-done.3
  92.2 3.3 %caches.1 = (bf16[24,16,2048]{2,1,0:T(8,128)(2,1)}, f32[3,16,1024]{2,1,0:T(8,128)}, bf16[3,3,1024]{2,1,0:T(4,128)(2,1)}) custom-call(s32[16]{0:T(128)S(1)} %copy-done.2, s32[16]{0:T(128)S(1)} %copy-done.3, s32[16,64]{1,0:T(8,128)S(1)} %copy-done.1, bf16[16,8,16,2048]{3,2,1,0:T(8,128)(2,1)} %all-gather.2.cloned.1.call-done.kv_ref, ...), custom_call_target="tpu_custom_call" | custom-call | tf_op jit(solution)/shard_map/caches/pallas_call | solution.py:450
Async XLA Ops:
  7.2 85.0 %all-gather.2.cloned.1.call-start = ((), (), s32[]{:S(2)}) async-start(), calls=%async_computation.3 | async-start | bytes 8912896 | tf_op jit(solution)/shard_map/all_gather | solution.py:498
  8.8 6.6 %collective-permute-start = (bf16[8,8192]{1,0:T(8,128)(2,1)S(1)}, bf16[8,8192]{1,0:T(8,128)(2,1)S(1)}, u32[]{:S(2)}, u32[]{:S(2)}) collective-permute-start(bf16[8,8192]{1,0:T(8,128)(2,1)S(1)} %slice_bitcast_fusion), channel_id=1, source_target_pairs={{0,16},{16,32},{32,48},{48,64},{64,80},{80,96},{96,112},{1,17},{17... | collective-permute-start | bytes 393224 | tf_op jit(solution)/shard_map/ppermute | solution.py:499
  15.5 0.7 copy-start.4
  16.1 38.2 %copy-start = (f32[16,8192]{1,0:T(8,128)S(1)}, f32[16,8192]{1,0:T(8,128)}, u32[]{:S(2)}) copy-start(f32[16,8192]{1,0:T(8,128)} %log_ref.5) | copy-start | bytes 1572868
  16.1 38.2 %copy-start.2 = (s32[16]{0:T(128)S(1)}, s32[16]{0:T(128)}, u32[]{:S(2)}) copy-start(s32[16]{0:T(128)} %dest_ref.3) | copy-start | bytes 196
  66.5 25.7 %all-to-all-start.2 = ((bf16[16,24,1024]{2,1,0:T(8,128)(2,1)}), bf16[16,24,1024]{2,1,0:T(8,128)(2,1)S(1)}, u32[]{:S(2)}, u32[]{:S(2)}) async-start(bf16[16,24,1024]{2,1,0:T(8,128)(2,1)} %get-tuple-element.22), calls=%async_computation.2 | async-start | bytes 1572864 | tf_op jit(solution)/shard_map/all_to_all | solution.py:518
  73.5 18.7 %copy-start.1 = (s32[16,64]{1,0:T(8,128)S(1)}, s32[16,64]{1,0:T(8,128)}, u32[]{:S(2)}) copy-start(s32[16,64]{1,0:T(8,128)} %slot_ref.1) | copy-start | bytes 12292
  73.5 18.7 %copy-start.3 = (s32[16]{0:T(128)S(1)}, s32[16]{0:T(128)}, u32[]{:S(2)}) copy-start(s32[16]{0:T(128)} %count_ref.7) | copy-start | bytes 196
Sparse Core Ops, SparseCore 0:
  10.1 79.7 all-gather.1

commit v5 on v3

--- a/solution.py
+++ b/solution.py
@@ -193,7 +193,7 @@
         msg_ref[(l * width) // piece, :, inside] = message.astype(BF16)
         return carry
 
-    lax.fori_loop(0, channels // width, tile, 0)
+    lax.fori_loop(0, channels // width, tile, 0, unroll=True)
 
 
 def local_scan(
@@ -364,33 +364,38 @@
     cache_ref,
     state_ref,
     rows_ref,
-    kv_sems,
+    zero_s,
+    used_s,
+    sem,
 ):
-    groups = got_ref.shape[0]
+    groups, capacity = got_ref.shape[0], cache_ref.shape[0]
     grp_pos = lax.axis_index("grp")
     first = lax.axis_index("seq") * here
-    cache_ref[...] = jnp.zeros_like(cache_ref)
-
-    def each_block(act):
-        def request(g, carry):
-            @pl.when(dest_ref[g] == grp_pos)
-            def _():
-                def block(j, carry):
+    for c in range(capacity):
+        used_s[c] = 0
+
+    def request(g, carry):
+        @pl.when(dest_ref[g] == grp_pos)
+        def _():
+            last = count_ref[g] - first
+            for j in range(here):
+
+                @pl.when(j < last)
+                def _():
                     slot = slot_ref[g, first + j]
-                    act(
-                        pltpu.make_async_copy(
-                            kv_ref.at[g, j], cache_ref.at[slot], kv_sems.at[slot]
-                        )
-                    )
-                    return carry
-
-                lax.fori_loop(0, jnp.clip(count_ref[g] - first, 0, here), block, 0)
-
-            return carry
-
-        lax.fori_loop(0, groups, request, 0)
-
-    each_block(lambda copy: copy.start())
+                    used_s[slot] = 1
+                    pltpu.make_async_copy(kv_ref.at[g, j], cache_ref.at[slot], sem).start()
+
+        return carry
+
+    lax.fori_loop(0, groups, request, 0)
+    zero_s[...] = jnp.zeros_like(zero_s)
+    for c in range(capacity):
+
+        @pl.when(used_s[c] == 0)
+        def _():
+            pltpu.make_async_copy(zero_s, cache_ref.at[c], sem).start()
+
     state_ref[...] = jnp.zeros_like(state_ref)
     rows_ref[...] = jnp.zeros_like(rows_ref)
 
@@ -406,7 +411,7 @@
         return taken + mine.astype(jnp.int32)
 
     lax.fori_loop(0, groups, one, jnp.int32(0))
-    each_block(lambda copy: copy.wait())
+    pltpu.make_async_copy(cache_ref, cache_ref, sem).wait()
 
 
 def caches(decode_device, block_count, block_slot, kv, got, here, capacity):
@@ -428,7 +433,9 @@
             jax.ShapeDtypeStruct((MOST, KCONV - 1, piece), BF16),
         ],
         scratch_shapes=[
-            pltpu.SemaphoreType.DMA((capacity,)),
+            pltpu.VMEM((BLOCK, width), BF16),
+            pltpu.SMEM((capacity,), jnp.int32),
+            pltpu.SemaphoreType.DMA,
         ],
         compiler_params=pltpu.CompilerParams(vmem_limit_bytes=WIDE_BYTES),
         name="caches",

time: 103 us -> 104 us (level)
  waiting for transfers between devices: 6.16 us -> 7.22 us
    pallas_call x1, Pallas kernels: 22 us -> 20.6 us  [local_scan(): pl.pallas_call(functools.partial(scan_kernel, width), grid=(steps,), in_s...]
    all_to_all x1, waiting for transfers between devices: 5.48 us -> 6.53 us  [per_device(): lax.all_to_all(final, 'grp', split_axis=0, concat_axis=0, tiled=True)]
  transfers between devices with their start and end apart: 3 -> 3, of which waited for: 1 -> 1; matrix products, arithmetic and copies ran while one was open for 1% -> 1% of each run, Pallas kernels for 41% -> 40%
where the time goes in v5:
time: 104 us; the launch traced here: 102 us
  Pallas kernels  44.2 us (42%)
  blocking collectives  26.7 us (26%)
  between operations  14.1 us (14%)
  starting transfers between devices  8.38 us (8%)
  waiting for transfers between devices  7.22 us (7%)
  local copies, waits for them, and re-layouts  1.59 us (2%)
    pallas_call x1, Pallas kernels, local_scan(): pl.pallas_call(functools.partial(scan_kernel, width), grid=(steps,), in_s...  20.6 us
    all_to_all x1, blocking collectives, per_device(): got = lax.all_to_all(msg, 'seq', split_axis=0, concat_axis=0, tiled=True)  16.1 us
    pallas_call x1, Pallas kernels, finish(): pl.pallas_call(functools.partial(finish_kernel, width), grid=(steps,), in...  13.3 us
    all_to_all x1, blocking collectives, per_device(): lax.all_to_all(starts, 'seq', split_axis=0, concat_axis=0, tiled=True)  10.6 us
    all_to_all x1, starting transfers between devices, per_device(): lax.all_to_all(final, 'grp', split_axis=0, concat_axis=0, tiled=True)  7.04 us
    all_to_all x1, waiting for transfers between devices, per_device(): lax.all_to_all(final, 'grp', split_axis=0, concat_axis=0, tiled=True)  6.53 us
    pallas_call x1, Pallas kernels, prepare(): pl.pallas_call(functools.partial(prepare_kernel, width), grid=(steps,), i...  5.33 us
    pallas_call x1, Pallas kernels, caches(): pl.pallas_call(functools.partial(caches_kernel, here), in_specs=[SM, SM,...  3.33 us
  transfers between devices with their start and end apart: 3, of which 1 were waited for; matrix products, arithmetic and copies ran while one was open for 1% of the time, Pallas kernels for 40%

profile of v5, /device:TPU:0, one launch (start us, length us, event | category | flops | bytes accessed | tf_op | source)
XLA Modules:
  0.0 102.2 jit_solution(2792299509097562431)
XLA Ops:
  7.2 0.0 all-gather.2.cloned.1.call-start
  7.2 0.7 all-gather.2.cloned.1.call-update
  7.9 0.9 slice_bitcast_fusion
  8.8 1.3 %collective-permute-start = (bf16[8,8192]{1,0:T(8,128)(2,1)S(1)}, bf16[8,8192]{1,0:T(8,128)(2,1)S(1)}, u32[]{:S(2)}, u32[]{:S(2)}) collective-permute-start(bf16[8,8192]{1,0:T(8,128)(2,1)S(1)} %slice_bitcast_fusion), channel_id=1, source_target_pairs={{0,16},{16,32},{32,48},{48,64},{64,80},{80,96},{96,112},{1,17},{17... | collective-permute-start | bytes 393224 | tf_op jit(solution)/shard_map/ppermute | solution.py:467
  10.1 5.3 %prepare.1 = (f32[8,16,8192]{2,1,0:T(8,128)}, f32[128,16,128]{2,1,0:T(8,128)}, bf16[8,16,256]{2,1,0:T(8,128)(2,1)}) custom-call(s32[16]{0:T(128)} %count_ref.7, bf16[128,8192]{1,0:T(8,128)(2,1)} %bitcast.16, f32[1,8192]{1,0:T(1,128)} %bitcast.20, bf16[2,16,128]{2,1,0:T(8,128)(2,1)} %bitcast.24), custom_call_target="tpu_custom_call" | custom-call | flops 20971520 | bytes 10485760 | tf_op jit(solution)/shard_map/prepare/pallas_call | solution.py:87
  15.5 0.0 collective-permute-done.halo_ref
  15.5 0.0 copy-start.4
  15.5 0.6 copy-done.4
  16.1 0.0 copy-start
  16.1 0.0 copy-start.2
  16.1 20.6 %local_scan.1 = (f32[8,16,8192]{2,1,0:T(8,128)}, f32[8,16,8192]{2,1,0:T(8,128)}, bf16[8,24,1024]{2,1,0:T(8,128)(2,1)}) custom-call(s32[16]{0:T(128)} %count_ref.7, bf16[128,8192]{1,0:T(8,128)(2,1)} %bitcast.15, bf16[8,8192]{1,0:T(8,128)(2,1)} %copy-done.4, f32[8,16,8192]{2,1,0:T(8,128)} %get-tuple-element.15.dt_ref, f32[16,8192]{1,0:T(8,128)} %log_ref.5, ...), custom_call_target="tpu_custom_call" | custom-call | flops 134217728 | bytes 12582912 | tf_op jit(solution)/shard_map/local_scan/pallas_call | solution.py:218
  36.7 16.1 %all_to_all.15.got_ref = bf16[8,24,1024]{2,1,0:T(8,128)(2,1)S(1)} all-to-all(bf16[8,24,1024]{2,1,0:T(8,128)(2,1)} %get-tuple-element.18), channel_id=1, replica_groups=mesh['seq'=8,'grp'=16] {'seq'}, dimensions={0} | all-to-all | bytes 786432 | tf_op jit(solution)/shard_map/all_to_all | solution.py:483
  52.9 0.0 copy-done
  52.9 0.0 copy-done.2
  52.9 1.6 %chain.1 = (bf16[8,16,1024]{2,1,0:T(8,128)(2,1)S(1)}, bf16[16,24,1024]{2,1,0:T(8,128)(2,1)}) custom-call(s32[16]{0:T(128)S(1)} %copy-done.2, bf16[8,24,1024]{2,1,0:T(8,128)(2,1)S(1)} %all_to_all.15.got_ref, f32[16,8192]{1,0:T(8,128)S(1)} %copy-done), custom_call_target="tpu_custom_call" | custom-call | tf_op jit(solution)/shard_map/chain/pallas_call | solution.py:274
  54.5 10.6 %all_to_all.16.start_ref = bf16[8,16,1024]{2,1,0:T(8,128)(2,1)} all-to-all(bf16[8,16,1024]{2,1,0:T(8,128)(2,1)S(1)} %get-tuple-element.19), channel_id=1, replica_groups=mesh['seq'=8,'grp'=16] {'seq'}, dimensions={0} | all-to-all | bytes 524288 | tf_op jit(solution)/shard_map/all_to_all | solution.py:485
  65.1 7.0 %all-to-all-start.2 = ((bf16[16,24,1024]{2,1,0:T(8,128)(2,1)}), bf16[16,24,1024]{2,1,0:T(8,128)(2,1)S(1)}, u32[]{:S(2)}, u32[]{:S(2)}) async-start(bf16[16,24,1024]{2,1,0:T(8,128)(2,1)} %get-tuple-element.22), calls=%async_computation.2 | async-start | bytes 1572864 | tf_op jit(solution)/shard_map/all_to_all | solution.py:486
  72.2 0.0 copy-start.1
  72.2 0.0 copy-start.3
  72.2 13.3 %finish.1 = bf16[128,8192]{1,0:T(8,128)(2,1)} custom-call(s32[16]{0:T(128)} %count_ref.7, bf16[8,16,1024]{2,1,0:T(8,128)(2,1)} %all_to_all.16.start_ref, f32[8,16,8192]{2,1,0:T(8,128)} %get-tuple-element.20.out_ref, f32[8,16,8192]{2,1,0:T(8,128)} %get-tuple-element.21.run_ref, f32[16,8192]{1,0:T(8,128)} %log_ref.5, bf16[128,8192]{1,0:T(8,128)(2,1)} %bitcast.17, ...), custom_call_target="tpu_custom_call" | custom-call | flops 67108864 | bytes 12582912 | tf_op jit(solution)/shard_map/finish/pallas_call | solution.py:332
  85.4 6.5 %all-to-all-done.2.got_ref = bf16[16,24,1024]{2,1,0:T(8,128)(2,1)S(1)} async-done(((bf16[16,24,1024]{2,1,0:T(8,128)(2,1)}), bf16[16,24,1024]{2,1,0:T(8,128)(2,1)S(1)}, u32[]{:S(2)}, u32[]{:S(2)}) %all-to-all-start.2) | async-done | bytes 786464 | tf_op jit(solution)/shard_map/all_to_all | solution.py:486
  92.0 0.0 all-gather.2.cloned.1.call-done.kv_ref
  92.0 0.0 copy-done.1
  92.0 0.0 copy-done.3
  92.0 3.3 %caches.1 = (bf16[24,16,2048]{2,1,0:T(8,128)(2,1)}, f32[3,16,1024]{2,1,0:T(8,128)}, bf16[3,3,1024]{2,1,0:T(4,128)(2,1)}) custom-call(s32[16]{0:T(128)S(1)} %copy-done.2, s32[16]{0:T(128)S(1)} %copy-done.3, s32[16,64]{1,0:T(8,128)S(1)} %copy-done.1, bf16[16,8,16,2048]{3,2,1,0:T(8,128)(2,1)} %all-gather.2.cloned.1.call-done.kv_ref, ...), custom_call_target="tpu_custom_call" | custom-call | tf_op jit(solution)/shard_map/caches/pallas_call | solution.py:420
Async XLA Ops:
  7.2 84.8 %all-gather.2.cloned.1.call-start = ((), (), s32[]{:S(2)}) async-start(), calls=%async_computation.3 | async-start | bytes 8912896 | tf_op jit(solution)/shard_map/all_gather | solution.py:466
  8.8 6.6 %collective-permute-start = (bf16[8,8192]{1,0:T(8,128)(2,1)S(1)}, bf16[8,8192]{1,0:T(8,128)(2,1)S(1)}, u32[]{:S(2)}, u32[]{:S(2)}) collective-permute-start(bf16[8,8192]{1,0:T(8,128)(2,1)S(1)} %slice_bitcast_fusion), channel_id=1, source_target_pairs={{0,16},{16,32},{32,48},{48,64},{64,80},{80,96},{96,112},{1,17},{17... | collective-permute-start | bytes 393224 | tf_op jit(solution)/shard_map/ppermute | solution.py:467
  15.5 0.7 copy-start.4
  16.1 36.8 %copy-start = (f32[16,8192]{1,0:T(8,128)S(1)}, f32[16,8192]{1,0:T(8,128)}, u32[]{:S(2)}) copy-start(f32[16,8192]{1,0:T(8,128)} %log_ref.5) | copy-start | bytes 1572868
  16.1 36.8 %copy-start.2 = (s32[16]{0:T(128)S(1)}, s32[16]{0:T(128)}, u32[]{:S(2)}) copy-start(s32[16]{0:T(128)} %dest_ref.3) | copy-start | bytes 196
  65.1 26.9 %all-to-all-start.2 = ((bf16[16,24,1024]{2,1,0:T(8,128)(2,1)}), bf16[16,24,1024]{2,1,0:T(8,128)(2,1)S(1)}, u32[]{:S(2)}, u32[]{:S(2)}) async-start(bf16[16,24,1024]{2,1,0:T(8,128)(2,1)} %get-tuple-element.22), calls=%async_computation.2 | async-start | bytes 1572864 | tf_op jit(solution)/shard_map/all_to_all | solution.py:486
  72.2 19.8 %copy-start.1 = (s32[16,64]{1,0:T(8,128)S(1)}, s32[16,64]{1,0:T(8,128)}, u32[]{:S(2)}) copy-start(s32[16,64]{1,0:T(8,128)} %slot_ref.1) | copy-start | bytes 12292
  72.2 19.8 %copy-start.3 = (s32[16]{0:T(128)S(1)}, s32[16]{0:T(128)}, u32[]{:S(2)}) copy-start(s32[16]{0:T(128)} %count_ref.7) | copy-start | bytes 196
Sparse Core Ops, SparseCore 0:
  10.1 80.5 all-gather.1

commit v6 on v3

--- a/solution.py
+++ b/solution.py
@@ -193,7 +193,7 @@
         msg_ref[(l * width) // piece, :, inside] = message.astype(BF16)
         return carry
 
-    lax.fori_loop(0, channels // width, tile, 0)
+    lax.fori_loop(0, channels // width, tile, 0, unroll=True)
 
 
 def local_scan(
@@ -266,7 +266,10 @@
         tails = tails + got[NSTATE:]
     final_ref[...] = jnp.zeros_like(final_ref)
     dest = dest_ref[lax.axis_index("grp")]
-    final_ref[dest] = jnp.concatenate([state, tails], axis=0).astype(BF16)
+    rows = tails[2 : 1 + KCONV]
+    packed = [state[:, lane : lane + LANES] for lane in range(0, piece, LANES)]
+    packed += [rows[:, lane : lane + LANES] for lane in range(0, piece, LANES)]
+    final_ref[dest] = jnp.concatenate(packed, axis=0).astype(BF16)
 
 
 def chain(decode_device, got, log, groups):
@@ -277,7 +280,7 @@
         out_specs=[VM(), VM()],
         out_shape=[
             jax.ShapeDtypeStruct((pieces, NSTATE, piece), BF16),
-            jax.ShapeDtypeStruct((groups, MSG, piece), BF16),
+            jax.ShapeDtypeStruct((groups, (NSTATE + KCONV - 1) * piece // LANES, LANES), BF16),
         ],
         compiler_params=pltpu.CompilerParams(vmem_limit_bytes=SMALL_BYTES),
         name="chain",
@@ -400,8 +403,12 @@
         @pl.when(mine)
         def _():
             got = got_ref[g].astype(F32)
-            state_ref[taken] = got[:NSTATE]
-            rows_ref[taken] = got[NSTATE + 2 : NSTATE + 1 + KCONV].astype(BF16)
+            parts = state_ref.shape[2] // LANES
+            tail = got[parts * NSTATE :]
+            state = [got[p * NSTATE : (p + 1) * NSTATE] for p in range(parts)]
+            rows = [tail[p * (KCONV - 1) : (p + 1) * (KCONV - 1)] for p in range(parts)]
+            state_ref[taken] = jnp.concatenate(state, axis=1)
+            rows_ref[taken] = jnp.concatenate(rows, axis=1).astype(BF16)
 
         return taken + mine.astype(jnp.int32)
 
@@ -409,8 +416,7 @@
     each_block(lambda copy: copy.wait())
 
 
-def caches(decode_device, block_count, block_slot, kv, got, here, capacity):
-    piece = got.shape[2]
+def caches(decode_device, block_count, block_slot, kv, got, here, capacity, piece):
     width = kv.shape[-1]
     return pl.pallas_call(
         functools.partial(caches_kernel, here),
@@ -479,7 +485,7 @@
     final_got = lax.all_to_all(final, "grp", split_axis=0, concat_axis=0, tiled=True)
     block_out = finish(block_count, start, out, run, decay_log, gate_input[0], c_diag, STEPS)
     kv_cache, ssm_cache, conv_cache = caches(
-        decode_device, block_count, block_slot, kv_all, final_got, here, MOST * here
+        decode_device, block_count, block_slot, kv_all, final_got, here, MOST * here, channels // pieces
     )
     return block_out[None], kv_cache[None, None], ssm_cache[None], conv_cache[None]
 

time: 103 us -> 102 us (level)
    pallas_call x1, Pallas kernels: 22 us -> 20.6 us  [local_scan(): pl.pallas_call(functools.partial(scan_kernel, width), grid=(steps,), in_s...]
    all_to_all x1, waiting for transfers between devices: 5.48 us -> 4.25 us  [per_device(): lax.all_to_all(final, 'grp', split_axis=0, concat_axis=0, tiled=True)]
  transfers between devices with their start and end apart: 3 -> 3, of which waited for: 1 -> 2; matrix products, arithmetic and copies ran while one was open for 1% -> 1% of each run, Pallas kernels for 41% -> 41%
where the time goes in v6:
time: 102 us; the launch traced here: 100 us
  Pallas kernels  44.4 us (44%)
  blocking collectives  26.7 us (26%)
  between operations  14.1 us (14%)
  starting transfers between devices  8.38 us (8%)
  waiting for transfers between devices  5.24 us (5%)
  local copies, waits for them, and re-layouts  1.59 us (2%)
    pallas_call x1, Pallas kernels, local_scan(): pl.pallas_call(functools.partial(scan_kernel, width), grid=(steps,), in_s...  20.6 us
    all_to_all x1, blocking collectives, per_device(): got = lax.all_to_all(msg, 'seq', split_axis=0, concat_axis=0, tiled=True)  16.1 us
    pallas_call x1, Pallas kernels, finish(): pl.pallas_call(functools.partial(finish_kernel, width), grid=(steps,), in...  13.3 us
    all_to_all x1, blocking collectives, per_device(): lax.all_to_all(starts, 'seq', split_axis=0, concat_axis=0, tiled=True)  10.6 us
    all_to_all x1, starting transfers between devices, per_device(): lax.all_to_all(final, 'grp', split_axis=0, concat_axis=0, tiled=True)  7.04 us
    pallas_call x1, Pallas kernels, prepare(): pl.pallas_call(functools.partial(prepare_kernel, width), grid=(steps,), i...  5.33 us
    all_to_all x1, waiting for transfers between devices, per_device(): lax.all_to_all(final, 'grp', split_axis=0, concat_axis=0, tiled=True)  4.25 us
    pallas_call x1, Pallas kernels, caches(): pl.pallas_call(functools.partial(caches_kernel, here), in_specs=[SM, SM,...  3.57 us
  transfers between devices with their start and end apart: 3, of which 2 were waited for; matrix products, arithmetic and copies ran while one was open for 1% of the time, Pallas kernels for 41%

profile of v6, /device:TPU:0, one launch (start us, length us, event | category | flops | bytes accessed | tf_op | source)
XLA Modules:
  0.0 100.4 jit_solution(4433761234094000192)
XLA Ops:
  7.2 0.0 all-gather.2.cloned.1.call-start
  7.2 0.7 all-gather.2.cloned.1.call-update
  7.9 0.9 slice_bitcast_fusion
  8.8 1.3 %collective-permute-start = (bf16[8,8192]{1,0:T(8,128)(2,1)S(1)}, bf16[8,8192]{1,0:T(8,128)(2,1)S(1)}, u32[]{:S(2)}, u32[]{:S(2)}) collective-permute-start(bf16[8,8192]{1,0:T(8,128)(2,1)S(1)} %slice_bitcast_fusion), channel_id=1, source_target_pairs={{0,16},{16,32},{32,48},{48,64},{64,80},{80,96},{96,112},{1,17},{17... | collective-permute-start | bytes 393224 | tf_op jit(solution)/shard_map/ppermute | solution.py:466
  10.1 5.3 %prepare.1 = (f32[8,16,8192]{2,1,0:T(8,128)}, f32[128,16,128]{2,1,0:T(8,128)}, bf16[8,16,256]{2,1,0:T(8,128)(2,1)}) custom-call(s32[16]{0:T(128)} %count_ref.7, bf16[128,8192]{1,0:T(8,128)(2,1)} %bitcast.16, f32[1,8192]{1,0:T(1,128)} %bitcast.20, bf16[2,16,128]{2,1,0:T(8,128)(2,1)} %bitcast.24), custom_call_target="tpu_custom_call" | custom-call | flops 20971520 | bytes 10485760 | tf_op jit(solution)/shard_map/prepare/pallas_call | solution.py:87
  15.5 0.0 collective-permute-done.halo_ref
  15.5 0.0 copy-start.4
  15.5 0.6 copy-done.4
  16.1 0.0 copy-start
  16.1 0.0 copy-start.2
  16.1 20.6 %local_scan.1 = (f32[8,16,8192]{2,1,0:T(8,128)}, f32[8,16,8192]{2,1,0:T(8,128)}, bf16[8,24,1024]{2,1,0:T(8,128)(2,1)}) custom-call(s32[16]{0:T(128)} %count_ref.7, bf16[128,8192]{1,0:T(8,128)(2,1)} %bitcast.15, bf16[8,8192]{1,0:T(8,128)(2,1)} %copy-done.4, f32[8,16,8192]{2,1,0:T(8,128)} %get-tuple-element.15.dt_ref, f32[16,8192]{1,0:T(8,128)} %log_ref.5, ...), custom_call_target="tpu_custom_call" | custom-call | flops 134217728 | bytes 12582912 | tf_op jit(solution)/shard_map/local_scan/pallas_call | solution.py:218
  36.7 16.1 %all_to_all.15.got_ref = bf16[8,24,1024]{2,1,0:T(8,128)(2,1)S(1)} all-to-all(bf16[8,24,1024]{2,1,0:T(8,128)(2,1)} %get-tuple-element.18), channel_id=1, replica_groups=mesh['seq'=8,'grp'=16] {'seq'}, dimensions={0} | all-to-all | bytes 786432 | tf_op jit(solution)/shard_map/all_to_all | solution.py:482
  52.9 0.0 copy-done
  52.9 0.0 copy-done.2
  52.9 1.6 %chain.1 = (bf16[8,16,1024]{2,1,0:T(8,128)(2,1)S(1)}, bf16[16,152,128]{2,1,0:T(8,128)(2,1)}) custom-call(s32[16]{0:T(128)S(1)} %copy-done.2, bf16[8,24,1024]{2,1,0:T(8,128)(2,1)S(1)} %all_to_all.15.got_ref, f32[16,8192]{1,0:T(8,128)S(1)} %copy-done), custom_call_target="tpu_custom_call" | custom-call | tf_op jit(solution)/shard_map/chain/pallas_call | solution.py:277
  54.5 10.6 %all_to_all.16.start_ref = bf16[8,16,1024]{2,1,0:T(8,128)(2,1)} all-to-all(bf16[8,16,1024]{2,1,0:T(8,128)(2,1)S(1)} %get-tuple-element.19), channel_id=1, replica_groups=mesh['seq'=8,'grp'=16] {'seq'}, dimensions={0} | all-to-all | bytes 524288 | tf_op jit(solution)/shard_map/all_to_all | solution.py:484
  65.1 7.0 %all-to-all-start.2 = ((bf16[16,152,128]{2,1,0:T(8,128)(2,1)}), bf16[16,152,128]{2,1,0:T(8,128)(2,1)S(1)}, u32[]{:S(2)}, u32[]{:S(2)}) async-start(bf16[16,152,128]{2,1,0:T(8,128)(2,1)} %get-tuple-element.22), calls=%async_computation.2 | async-start | bytes 1245184 | tf_op jit(solution)/shard_map/all_to_all | solution.py:485
  72.1 0.0 copy-start.1
  72.2 0.0 copy-start.3
  72.2 13.3 %finish.1 = bf16[128,8192]{1,0:T(8,128)(2,1)} custom-call(s32[16]{0:T(128)} %count_ref.7, bf16[8,16,1024]{2,1,0:T(8,128)(2,1)} %all_to_all.16.start_ref, f32[8,16,8192]{2,1,0:T(8,128)} %get-tuple-element.20.out_ref, f32[8,16,8192]{2,1,0:T(8,128)} %get-tuple-element.21.run_ref, f32[16,8192]{1,0:T(8,128)} %log_ref.5, bf16[128,8192]{1,0:T(8,128)(2,1)} %bitcast.17, ...), custom_call_target="tpu_custom_call" | custom-call | flops 67108864 | bytes 12582912 | tf_op jit(solution)/shard_map/finish/pallas_call | solution.py:335
  85.4 4.3 %all-to-all-done.2.got_ref = bf16[16,152,128]{2,1,0:T(8,128)(2,1)S(1)} async-done(((bf16[16,152,128]{2,1,0:T(8,128)(2,1)}), bf16[16,152,128]{2,1,0:T(8,128)(2,1)S(1)}, u32[]{:S(2)}, u32[]{:S(2)}) %all-to-all-start.2) | async-done | bytes 622624 | tf_op jit(solution)/shard_map/all_to_all | solution.py:485
  89.7 0.3 all-gather.2.cloned.1.call-done.kv_ref
  90.0 0.0 copy-done.1
  90.0 0.0 copy-done.3
  90.0 3.6 %caches.1 = (bf16[24,16,2048]{2,1,0:T(8,128)(2,1)}, f32[3,16,1024]{2,1,0:T(8,128)}, bf16[3,3,1024]{2,1,0:T(4,128)(2,1)}) custom-call(s32[16]{0:T(128)S(1)} %copy-done.2, s32[16]{0:T(128)S(1)} %copy-done.3, s32[16,64]{1,0:T(8,128)S(1)} %copy-done.1, bf16[16,8,16,2048]{3,2,1,0:T(8,128)(2,1)} %all-gather.2.cloned.1.call-done.kv_ref, ...), custom_call_target="tpu_custom_call" | custom-call | tf_op jit(solution)/shard_map/caches/pallas_call | solution.py:421
Async XLA Ops:
  7.2 82.8 %all-gather.2.cloned.1.call-start = ((), (), s32[]{:S(2)}) async-start(), calls=%async_computation.3 | async-start | bytes 8912896 | tf_op jit(solution)/shard_map/all_gather | solution.py:465
  8.8 6.6 %collective-permute-start = (bf16[8,8192]{1,0:T(8,128)(2,1)S(1)}, bf16[8,8192]{1,0:T(8,128)(2,1)S(1)}, u32[]{:S(2)}, u32[]{:S(2)}) collective-permute-start(bf16[8,8192]{1,0:T(8,128)(2,1)S(1)} %slice_bitcast_fusion), channel_id=1, source_target_pairs={{0,16},{16,32},{32,48},{48,64},{64,80},{80,96},{96,112},{1,17},{17... | collective-permute-start | bytes 393224 | tf_op jit(solution)/shard_map/ppermute | solution.py:466
  15.5 0.7 copy-start.4
  16.1 36.8 %copy-start = (f32[16,8192]{1,0:T(8,128)S(1)}, f32[16,8192]{1,0:T(8,128)}, u32[]{:S(2)}) copy-start(f32[16,8192]{1,0:T(8,128)} %log_ref.5) | copy-start | bytes 1572868
  16.1 36.8 %copy-start.2 = (s32[16]{0:T(128)S(1)}, s32[16]{0:T(128)}, u32[]{:S(2)}) copy-start(s32[16]{0:T(128)} %dest_ref.3) | copy-start | bytes 196
  65.1 24.6 %all-to-all-start.2 = ((bf16[16,152,128]{2,1,0:T(8,128)(2,1)}), bf16[16,152,128]{2,1,0:T(8,128)(2,1)S(1)}, u32[]{:S(2)}, u32[]{:S(2)}) async-start(bf16[16,152,128]{2,1,0:T(8,128)(2,1)} %get-tuple-element.22), calls=%async_computation.2 | async-start | bytes 1245184 | tf_op jit(solution)/shard_map/all_to_all | solution.py:485
  72.1 17.8 %copy-start.1 = (s32[16,64]{1,0:T(8,128)S(1)}, s32[16,64]{1,0:T(8,128)}, u32[]{:S(2)}) copy-start(s32[16,64]{1,0:T(8,128)} %slot_ref.1) | copy-start | bytes 12292
  72.2 17.8 %copy-start.3 = (s32[16]{0:T(128)S(1)}, s32[16]{0:T(128)}, u32[]{:S(2)}) copy-start(s32[16]{0:T(128)} %count_ref.7) | copy-start | bytes 196
Sparse Core Ops, SparseCore 0:
  10.1 79.7 all-gather.1

commit v7 on v6

--- a/solution.py
+++ b/solution.py
@@ -391,7 +391,7 @@
 
             return carry
 
-        lax.fori_loop(0, groups, request, 0)
+        lax.fori_loop(0, groups, request, 0, unroll=True)
 
     each_block(lambda copy: copy.start())
     state_ref[...] = jnp.zeros_like(state_ref)
@@ -412,7 +412,7 @@
 
         return taken + mine.astype(jnp.int32)
 
-    lax.fori_loop(0, groups, one, jnp.int32(0))
+    lax.fori_loop(0, groups, one, jnp.int32(0), unroll=True)
     each_block(lambda copy: copy.wait())
 
 

time: 102 us -> 101 us (level)
  no operation moved by 1% of the time
where the time goes in v7:
time: 101 us; the launch traced here: 100 us
  Pallas kernels  44 us (44%)
  blocking collectives  26.7 us (26%)
  between operations  14.1 us (14%)
  starting transfers between devices  8.38 us (8%)
  waiting for transfers between devices  5.24 us (5%)
  local copies, waits for them, and re-layouts  1.59 us (2%)
    pallas_call x1, Pallas kernels, local_scan(): pl.pallas_call(functools.partial(scan_kernel, width), grid=(steps,), in_s...  20.6 us
    all_to_all x1, blocking collectives, per_device(): got = lax.all_to_all(msg, 'seq', split_axis=0, concat_axis=0, tiled=True)  16.1 us
    pallas_call x1, Pallas kernels, finish(): pl.pallas_call(functools.partial(finish_kernel, width), grid=(steps,), in...  13.3 us
    all_to_all x1, blocking collectives, per_device(): lax.all_to_all(starts, 'seq', split_axis=0, concat_axis=0, tiled=True)  10.6 us
    all_to_all x1, starting transfers between devices, per_device(): lax.all_to_all(final, 'grp', split_axis=0, concat_axis=0, tiled=True)  7.04 us
    pallas_call x1, Pallas kernels, prepare(): pl.pallas_call(functools.partial(prepare_kernel, width), grid=(steps,), i...  5.33 us
    all_to_all x1, waiting for transfers between devices, per_device(): lax.all_to_all(final, 'grp', split_axis=0, concat_axis=0, tiled=True)  4.25 us
    pallas_call x1, Pallas kernels, caches(): pl.pallas_call(functools.partial(caches_kernel, here), in_specs=[SM, SM,...  3.24 us
  transfers between devices with their start and end apart: 3, of which 2 were waited for; matrix products, arithmetic and copies ran while one was open for 1% of the time, Pallas kernels for 41%

profile of v7, /device:TPU:0, one launch (start us, length us, event | category | flops | bytes accessed | tf_op | source)
XLA Modules:
  0.0 100.1 jit_solution(12699320304969803472)
XLA Ops:
  7.2 0.0 all-gather.2.cloned.1.call-start
  7.2 0.7 all-gather.2.cloned.1.call-update
  7.9 0.9 slice_bitcast_fusion
  8.8 1.3 %collective-permute-start = (bf16[8,8192]{1,0:T(8,128)(2,1)S(1)}, bf16[8,8192]{1,0:T(8,128)(2,1)S(1)}, u32[]{:S(2)}, u32[]{:S(2)}) collective-permute-start(bf16[8,8192]{1,0:T(8,128)(2,1)S(1)} %slice_bitcast_fusion), channel_id=1, source_target_pairs={{0,16},{16,32},{32,48},{48,64},{64,80},{80,96},{96,112},{1,17},{17... | collective-permute-start | bytes 393224 | tf_op jit(solution)/shard_map/ppermute | solution.py:466
  10.1 5.3 %prepare.1 = (f32[8,16,8192]{2,1,0:T(8,128)}, f32[128,16,128]{2,1,0:T(8,128)}, bf16[8,16,256]{2,1,0:T(8,128)(2,1)}) custom-call(s32[16]{0:T(128)} %count_ref.7, bf16[128,8192]{1,0:T(8,128)(2,1)} %bitcast.16, f32[1,8192]{1,0:T(1,128)} %bitcast.20, bf16[2,16,128]{2,1,0:T(8,128)(2,1)} %bitcast.24), custom_call_target="tpu_custom_call" | custom-call | flops 20971520 | bytes 10485760 | tf_op jit(solution)/shard_map/prepare/pallas_call | solution.py:87
  15.5 0.0 collective-permute-done.halo_ref
  15.5 0.0 copy-start.4
  15.5 0.6 copy-done.4
  16.1 0.0 copy-start
  16.1 0.0 copy-start.2
  16.1 20.6 %local_scan.1 = (f32[8,16,8192]{2,1,0:T(8,128)}, f32[8,16,8192]{2,1,0:T(8,128)}, bf16[8,24,1024]{2,1,0:T(8,128)(2,1)}) custom-call(s32[16]{0:T(128)} %count_ref.7, bf16[128,8192]{1,0:T(8,128)(2,1)} %bitcast.15, bf16[8,8192]{1,0:T(8,128)(2,1)} %copy-done.4, f32[8,16,8192]{2,1,0:T(8,128)} %get-tuple-element.15.dt_ref, f32[16,8192]{1,0:T(8,128)} %log_ref.5, ...), custom_call_target="tpu_custom_call" | custom-call | flops 134217728 | bytes 12582912 | tf_op jit(solution)/shard_map/local_scan/pallas_call | solution.py:218
  36.7 16.1 %all_to_all.15.got_ref = bf16[8,24,1024]{2,1,0:T(8,128)(2,1)S(1)} all-to-all(bf16[8,24,1024]{2,1,0:T(8,128)(2,1)} %get-tuple-element.18), channel_id=1, replica_groups=mesh['seq'=8,'grp'=16] {'seq'}, dimensions={0} | all-to-all | bytes 786432 | tf_op jit(solution)/shard_map/all_to_all | solution.py:482
  52.9 0.0 copy-done
  52.9 0.0 copy-done.2
  52.9 1.6 %chain.1 = (bf16[8,16,1024]{2,1,0:T(8,128)(2,1)S(1)}, bf16[16,152,128]{2,1,0:T(8,128)(2,1)}) custom-call(s32[16]{0:T(128)S(1)} %copy-done.2, bf16[8,24,1024]{2,1,0:T(8,128)(2,1)S(1)} %all_to_all.15.got_ref, f32[16,8192]{1,0:T(8,128)S(1)} %copy-done), custom_call_target="tpu_custom_call" | custom-call | tf_op jit(solution)/shard_map/chain/pallas_call | solution.py:277
  54.5 10.6 %all_to_all.16.start_ref = bf16[8,16,1024]{2,1,0:T(8,128)(2,1)} all-to-all(bf16[8,16,1024]{2,1,0:T(8,128)(2,1)S(1)} %get-tuple-element.19), channel_id=1, replica_groups=mesh['seq'=8,'grp'=16] {'seq'}, dimensions={0} | all-to-all | bytes 524288 | tf_op jit(solution)/shard_map/all_to_all | solution.py:484
  65.1 7.0 %all-to-all-start.2 = ((bf16[16,152,128]{2,1,0:T(8,128)(2,1)}), bf16[16,152,128]{2,1,0:T(8,128)(2,1)S(1)}, u32[]{:S(2)}, u32[]{:S(2)}) async-start(bf16[16,152,128]{2,1,0:T(8,128)(2,1)} %get-tuple-element.22), calls=%async_computation.2 | async-start | bytes 1245184 | tf_op jit(solution)/shard_map/all_to_all | solution.py:485
  72.1 0.0 copy-start.1
  72.2 0.0 copy-start.3
  72.2 13.3 %finish.1 = bf16[128,8192]{1,0:T(8,128)(2,1)} custom-call(s32[16]{0:T(128)} %count_ref.7, bf16[8,16,1024]{2,1,0:T(8,128)(2,1)} %all_to_all.16.start_ref, f32[8,16,8192]{2,1,0:T(8,128)} %get-tuple-element.20.out_ref, f32[8,16,8192]{2,1,0:T(8,128)} %get-tuple-element.21.run_ref, f32[16,8192]{1,0:T(8,128)} %log_ref.5, bf16[128,8192]{1,0:T(8,128)(2,1)} %bitcast.17, ...), custom_call_target="tpu_custom_call" | custom-call | flops 67108864 | bytes 12582912 | tf_op jit(solution)/shard_map/finish/pallas_call | solution.py:335
  85.4 4.3 %all-to-all-done.2.got_ref = bf16[16,152,128]{2,1,0:T(8,128)(2,1)S(1)} async-done(((bf16[16,152,128]{2,1,0:T(8,128)(2,1)}), bf16[16,152,128]{2,1,0:T(8,128)(2,1)S(1)}, u32[]{:S(2)}, u32[]{:S(2)}) %all-to-all-start.2) | async-done | bytes 622624 | tf_op jit(solution)/shard_map/all_to_all | solution.py:485
  89.7 0.3 all-gather.2.cloned.1.call-done.kv_ref
  90.0 0.0 copy-done.1
  90.0 0.0 copy-done.3
  90.0 3.2 %caches.1 = (bf16[24,16,2048]{2,1,0:T(8,128)(2,1)}, f32[3,16,1024]{2,1,0:T(8,128)}, bf16[3,3,1024]{2,1,0:T(4,128)(2,1)}) custom-call(s32[16]{0:T(128)S(1)} %copy-done.2, s32[16]{0:T(128)S(1)} %copy-done.3, s32[16,64]{1,0:T(8,128)S(1)} %copy-done.1, bf16[16,8,16,2048]{3,2,1,0:T(8,128)(2,1)} %all-gather.2.cloned.1.call-done.kv_ref, ...), custom_call_target="tpu_custom_call" | custom-call | tf_op jit(solution)/shard_map/caches/pallas_call | solution.py:421
Async XLA Ops:
  7.2 82.8 %all-gather.2.cloned.1.call-start = ((), (), s32[]{:S(2)}) async-start(), calls=%async_computation.3 | async-start | bytes 8912896 | tf_op jit(solution)/shard_map/all_gather | solution.py:465
  8.8 6.6 %collective-permute-start = (bf16[8,8192]{1,0:T(8,128)(2,1)S(1)}, bf16[8,8192]{1,0:T(8,128)(2,1)S(1)}, u32[]{:S(2)}, u32[]{:S(2)}) collective-permute-start(bf16[8,8192]{1,0:T(8,128)(2,1)S(1)} %slice_bitcast_fusion), channel_id=1, source_target_pairs={{0,16},{16,32},{32,48},{48,64},{64,80},{80,96},{96,112},{1,17},{17... | collective-permute-start | bytes 393224 | tf_op jit(solution)/shard_map/ppermute | solution.py:466
  15.5 0.7 copy-start.4
  16.1 36.8 %copy-start = (f32[16,8192]{1,0:T(8,128)S(1)}, f32[16,8192]{1,0:T(8,128)}, u32[]{:S(2)}) copy-start(f32[16,8192]{1,0:T(8,128)} %log_ref.5) | copy-start | bytes 1572868
  16.1 36.8 %copy-start.2 = (s32[16]{0:T(128)S(1)}, s32[16]{0:T(128)}, u32[]{:S(2)}) copy-start(s32[16]{0:T(128)} %dest_ref.3) | copy-start | bytes 196
  65.1 24.6 %all-to-all-start.2 = ((bf16[16,152,128]{2,1,0:T(8,128)(2,1)}), bf16[16,152,128]{2,1,0:T(8,128)(2,1)S(1)}, u32[]{:S(2)}, u32[]{:S(2)}) async-start(bf16[16,152,128]{2,1,0:T(8,128)(2,1)} %get-tuple-element.22), calls=%async_computation.2 | async-start | bytes 1245184 | tf_op jit(solution)/shard_map/all_to_all | solution.py:485
  72.1 17.8 %copy-start.1 = (s32[16,64]{1,0:T(8,128)S(1)}, s32[16,64]{1,0:T(8,128)}, u32[]{:S(2)}) copy-start(s32[16,64]{1,0:T(8,128)} %slot_ref.1) | copy-start | bytes 12292
  72.2 17.8 %copy-start.3 = (s32[16]{0:T(128)S(1)}, s32[16]{0:T(128)}, u32[]{:S(2)}) copy-start(s32[16]{0:T(128)} %count_ref.7) | copy-start | bytes 196
Sparse Core Ops, SparseCore 0:
  10.1 79.7 all-gather.1
